TPU v7x, 512 devices: a whole 4x4x16 slice. The times are simulated.
512 devices in a mesh: inner: 16 (over z_hi, y, core), outer: 32 (over x, z_lo).
Axes of the slice: x: 4, y: 4, z: 16 (z_hi: 2, z_lo: 8; z = z_hi * 8 + z_lo), core: 2. Of those that a mesh axis runs over, the one named last changes fastest.
Arguments:
- queries: bfloat16 [131072, 4096], P(('inner', 'outer')), may hold values from -128 to 128
- keys: bfloat16 [131072, 512], P(('inner', 'outer')), may hold values from -6 to 6
- values: bfloat16 [131072, 512], P(('inner', 'outer')), may hold values from -6 to 6
- spans: int32 [512, 2], replicated, may hold values from 0 to 1023, as said below
Outputs:
- attended: bfloat16 [131072, 4096], P(('inner', 'outer'))
- log_sum: float32 [32, 131072], P(None, ('inner', 'outer'))
Inputs may be any that keep to these rules, and one draw needn't show every extreme that they name: `spans`: row d is c and 1023 - c, and every c of 0 to 511 appears in exactly one row.
All inputs are finite; a program needn't handle non-finite values.
Results may differ from a plain program's by a relative error of at most 0.0038.
Values may be sent and summed in bfloat16 or wider, within the bound.
No kernel may reach another device: no remote copies, remote signals or barrier semaphores. Data moves between devices by JAX's collectives and lax.ppermute only.
A program may use at most 128 MiB of HBM per device.

v0:
```python
import jax
import jax.numpy as jnp
from jax import lax
from jax.sharding import PartitionSpec as P

KEY_VALUE_HEADS = 4
HEAD_SIZE = 128


def passed_along(block, axis, distance):
    devices = range(lax.axis_size(axis))
    route = [((i - distance) % len(devices), i) for i in devices]
    return lax.ppermute(block, axis, route)


def block_positions(spans, source, row_total):
    pair = lax.dynamic_index_in_dim(spans, source, 0, keepdims=False)
    offsets = jnp.arange(row_total, dtype=jnp.int32)
    half_rows = row_total // 2
    first = jnp.where(offsets < half_rows, pair[0], pair[1])
    return first * half_rows + offsets % half_rows


def local(queries, keys, values, spans):
    row_total = queries.shape[0]
    n_inner = lax.axis_size("inner")
    n_outer = lax.axis_size("outer")
    inner_at = lax.axis_index("inner")
    outer_at = lax.axis_index("outer")
    near_keys, near_values = passed_along((keys, values), "inner", 1)
    far_keys, far_values = passed_along((near_keys, near_values), "inner", 1)
    side_keys, side_values = passed_along((keys, values), "outer", 1)
    source_devices = [
        inner_at * n_outer + outer_at,
        (inner_at - 1) % n_inner * n_outer + outer_at,
        (inner_at - 2) % n_inner * n_outer + outer_at,
        inner_at * n_outer + (outer_at - 1) % n_outer,
    ]
    query_pos = block_positions(spans, source_devices[0], row_total)
    window_pos = jnp.concatenate(
        [block_positions(spans, source, row_total) for source in source_devices]
    )
    live = window_pos[None, None, :] <= query_pos[None, :, None]
    windowed_keys = jnp.concatenate([keys, near_keys, far_keys, side_keys], axis=0)
    windowed_values = jnp.concatenate([values, near_values, far_values, side_values], axis=0)
    query_group = queries.shape[1] // (KEY_VALUE_HEADS * HEAD_SIZE)
    scale = HEAD_SIZE ** (-0.5)
    results = []
    logs = []
    for head_number in range(KEY_VALUE_HEADS):
        head_q = queries[
            :, head_number * query_group * HEAD_SIZE : (head_number + 1) * query_group * HEAD_SIZE
        ].reshape(row_total, query_group, HEAD_SIZE)
        head_k = windowed_keys[:, head_number * HEAD_SIZE : (head_number + 1) * HEAD_SIZE]
        head_v = windowed_values[:, head_number * HEAD_SIZE : (head_number + 1) * HEAD_SIZE]
        scores = (
            jnp.einsum("rgd,kd->grk", head_q, head_k, preferred_element_type=jnp.float32) * scale
        )
        scores = jnp.where(live, scores, -jnp.inf)
        top = jnp.max(scores, axis=-1)
        expo = jnp.exp(scores - top[..., None])
        total = jnp.sum(expo, axis=-1)
        weights = expo.astype(jnp.bfloat16)
        summed = jnp.einsum("grk,kd->rgd", weights, head_v, preferred_element_type=jnp.float32)
        result = summed / jnp.transpose(total)[:, :, None]
        results.append(result.reshape(row_total, query_group * HEAD_SIZE).astype(jnp.bfloat16))
        logs.append(top + jnp.log(total))
    return (jnp.concatenate(results, axis=1), jnp.concatenate(logs, axis=0))


def solution(mesh):
    placed = (
        P(("inner", "outer"), None),
        P(("inner", "outer"), None),
        P(("inner", "outer"), None),
        P(),
    )
    return jax.shard_map(
        local,
        mesh=mesh,
        in_specs=placed,
        out_specs=(P(("inner", "outer"), None), P(None, ("inner", "outer"))),
        check_vma=False,
    )
```

profile of v0, /device:TPU:217, one launch (start us, length us, event | category | flops | bytes accessed | tf_op | source)
XLA Modules:
  0.0 120.2 jit_solution(15516806721676582638)
XLA Ops:
  0.6 9.1 %collective-permute-start.3 = (bf16[256,512]{1,0:T(8,128)(2,1)}, bf16[256,512]{1,0:T(8,128)(2,1)}, u32[]{:S(2)}, u32[]{:S(2)}) collective-permute-start(bf16[256,512]{1,0:T(8,128)(2,1)} %param.5), channel_id=1, source_target_pairs={{480,0},{0,32},{32,64},{64,96},{96,128},{128,160},{160,192},{192,2... | collective-permute-start | bytes 786440 | tf_op jit(solution)/shard_map/ppermute | solution.py:13
  9.7 2.6 %collective-permute-start.5 = (bf16[256,512]{1,0:T(8,128)(2,1)}, bf16[256,512]{1,0:T(8,128)(2,1)S(1)}, u32[]{:S(2)}, u32[]{:S(2)}) collective-permute-start(bf16[256,512]{1,0:T(8,128)(2,1)} %param.5), channel_id=1, source_target_pairs={{31,0},{0,1},{1,2},{2,3},{3,4},{4,5},{5,6},{6,7},{7,8},{8,9},{9,10... | collective-permute-start | bytes 786440 | tf_op jit(solution)/shard_map/ppermute | solution.py:13
  12.4 1.1 copy.19
  13.4 7.4 %collective-permute-start.2 = (bf16[256,512]{0,1:T(8,128)(2,1)S(1)}, bf16[256,512]{0,1:T(8,128)(2,1)}, u32[]{:S(2)}, u32[]{:S(2)}) collective-permute-start(bf16[256,512]{0,1:T(8,128)(2,1)S(1)} %copy.19), channel_id=1, source_target_pairs={{31,0},{0,1},{1,2},{2,3},{3,4},{4,5},{5,6},{6,7},{7,8},{8,9},{9,10... | collective-permute-start | bytes 786440 | tf_op jit(solution)/shard_map/ppermute | solution.py:13
  20.9 2.5 %collective-permute-start = (bf16[256,512]{0,1:T(8,128)(2,1)S(1)}, bf16[256,512]{0,1:T(8,128)(2,1)}, u32[]{:S(2)}, u32[]{:S(2)}) collective-permute-start(bf16[256,512]{0,1:T(8,128)(2,1)S(1)} %copy.19), channel_id=1, source_target_pairs={{480,0},{0,32},{32,64},{64,96},{96,128},{128,160},{160,192},{192,2... | collective-permute-start | bytes 786440 | tf_op jit(solution)/shard_map/ppermute | solution.py:13
  23.4 0.9 constant_dynamic-slice_fusion.2
  24.4 0.6 fusion.59
  24.9 0.6 fusion.58
  25.5 0.6 fusion.57
  26.1 1.3 %multiply_add_fusion.3 = s32[256]{0:T(256)S(1)} fusion(s32[]{:T(128)} %bitcast.2, s32[]{:T(128)} %bitcast.1), kind=kLoop, calls=%fused_computation.65 | loop fusion | flops 2560 | bytes 1032 | tf_op jit(solution)/shard_map/add | solution.py:21
  27.4 1.3 %multiply_add_fusion.2 = s32[256]{0:T(256)S(1)} fusion(s32[]{:T(128)} %bitcast.4, s32[]{:T(128)} %bitcast.3), kind=kLoop, calls=%fused_computation.64 | loop fusion | flops 2560 | bytes 1032 | tf_op jit(solution)/shard_map/add | solution.py:21
  28.7 2.4 %multiply_add_fusion = (s32[256]{0:T(256)S(1)}, s32[256]{0:T(256)S(1)}) fusion(s32[]{:T(128)} %bitcast.8, s32[]{:T(128)} %bitcast.7, s32[]{:T(128)} %bitcast.6, s32[]{:T(128)} %bitcast.5), kind=kLoop, calls=%fused_computation.62 | loop fusion | flops 3328 | bytes 2064 | tf_op jit(solution)/shard_map/add | solution.py:21
  31.1 1.7 %fusion.56 = (bf16[256,1024]{1,0:T(8,128)(2,1)S(1)}, bf16[256,1024]{1,0:T(8,128)(2,1)S(1)}, bf16[256,1024]{1,0:T(8,128)(2,1)S(1)}, bf16[256,1024]{1,0:T(8,128)(2,1)S(1)}) fusion(bf16[256,4096]{1,0:T(8,128)(2,1)} %param.4), kind=kLoop, calls=%fused_computation.79 | loop fusion | bytes 4194304 | tf_op jit(solution)/shard_map/slice | solution.py:51
  32.8 0.0 collective-permute-done.3
  32.8 6.1 %collective-permute-start.4 = (bf16[256,512]{1,0:T(8,128)(2,1)}, bf16[256,512]{1,0:T(8,128)(2,1)}, u32[]{:S(2)}, u32[]{:S(2)}) collective-permute-start(bf16[256,512]{1,0:T(8,128)(2,1)} %collective-permute-done.3), channel_id=1, source_target_pairs={{480,0},{0,32},{32,64},{64,96},{96,128},{128,160},{160,192},{192,2... | collective-permute-start | bytes 786440 | tf_op jit(solution)/shard_map/ppermute | solution.py:13
  38.9 0.2 broadcast_compare_fusion
  39.2 1.7 %constant_dynamic-update-slice_fusion.3 = bf16[1024,512]{1,0:T(8,128)(2,1)} fusion(bf16[256,512]{1,0:T(8,128)(2,1)} %param.5), kind=kLoop, calls=%fused_computation.55 | loop fusion | bytes 524288
  40.8 0.2 copy.47
  41.0 0.2 copy.44
  41.2 0.2 copy.46
  41.5 1.0 copy.45
  42.4 8.9 %collective-permute-done = bf16[256,512]{0,1:T(8,128)(2,1)} collective-permute-done((bf16[256,512]{0,1:T(8,128)(2,1)S(1)}, bf16[256,512]{0,1:T(8,128)(2,1)}, u32[]{:S(2)}, u32[]{:S(2)}) %collective-permute-start) | collective-permute-done | bytes 262176 | tf_op jit(solution)/shard_map/ppermute | solution.py:13
  51.3 15.6 %collective-permute-start.1 = (bf16[256,512]{0,1:T(8,128)(2,1)}, bf16[256,512]{0,1:T(8,128)(2,1)S(1)}, u32[]{:S(2)}, u32[]{:S(2)}) collective-permute-start(bf16[256,512]{0,1:T(8,128)(2,1)} %collective-permute-done), channel_id=1, source_target_pairs={{480,0},{0,32},{32,64},{64,96},{96,128},{128,160},{160,192},{192,2... | collective-permute-start | bytes 786440 | tf_op jit(solution)/shard_map/ppermute | solution.py:13
  66.9 1.7 %constant_dynamic-update-slice_fusion.2 = bf16[1024,512]{1,0:T(8,128)(2,1)} fusion(bf16[1024,512]{1,0:T(8,128)(2,1)} %constant_dynamic-update-slice_fusion.3, bf16[256,512]{1,0:T(8,128)(2,1)} %collective-permute-done.3), kind=kLoop, calls=%fused_computation.54 | loop fusion | bytes 524288
  68.6 0.0 collective-permute-done.4
  68.6 1.7 %constant_dynamic-update-slice_fusion.1 = bf16[1024,512]{1,0:T(8,128)(2,1)} fusion(bf16[1024,512]{1,0:T(8,128)(2,1)} %constant_dynamic-update-slice_fusion.2, bf16[256,512]{1,0:T(8,128)(2,1)} %collective-permute-done.4), kind=kLoop, calls=%fused_computation.53 | loop fusion | bytes 524288
  70.3 0.0 collective-permute-done.5
  70.3 0.7 constant_dynamic-update-slice_fusion
  71.0 2.3 %fusion.44 = f32[1024,256,8]{1,0,2:T(8,128)S(1)} fusion(bf16[256,8,128]{0,2,1:T(8,128)(2,1)S(1)} %bitcast.120, bf16[1024,512]{1,0:T(8,128)(2,1)} %constant_dynamic-update-slice_fusion), kind=kOutput, calls=%fused_computation.40 | convolution fusion | flops 536870912 | bytes 9175040 | tf_op jit(solution)/shard_map/rgd,kd->grk/dot_general | solution.py:57
  73.3 1.2 %fusion.45 = f32[1024,256,8]{1,0,2:T(8,128)S(1)} fusion(bf16[256,8,128]{0,2,1:T(8,128)(2,1)S(1)} %bitcast.121, bf16[1024,512]{1,0:T(8,128)(2,1)S(1)} %copy-done.1), kind=kOutput, calls=%fused_computation.43 | convolution fusion | flops 536870912 | bytes 9175040 | tf_op jit(solution)/shard_map/rgd,kd->grk/dot_general | solution.py:57
  74.5 0.0 copy-start
  74.6 5.0 %fusion.8 = (f32[8,256]{1,0:T(8,128)S(1)}, f32[1024,256,8]{1,0,2:T(8,128)}) fusion(pred[256,1024]{0,1:T(8,128)(4,1)S(1)} %broadcast_compare_fusion, bf16[256,8,128]{0,2,1:T(8,128)(2,1)S(1)} %bitcast.122, bf16[1024,512]{1,0:T(8,128)(2,1)S(1)} %copy-done.1), kind=kOutput, calls=%fused_computation.16 | convolution fusion | flops 543160320 | bytes 9445376 | tf_op jit(solution)/shard_map/rgd,kd->grk/dot_general | solution.py:57
  79.5 0.0 copy-done.2
  79.5 9.9 %fusion = (f32[8,256]{1,0:T(8,128)S(1)}, f32[8,256]{1,0:T(8,128)S(1)}, f32[8,256]{1,0:T(8,128)S(1)}, f32[8,256]{1,0:T(8,128)S(1)}, f32[1024,256,8]{1,0,2:T(8,128)}) fusion(f32[1024,256,8]{1,0,2:T(8,128)} %get-tuple-element.26, f32[8,256]{1,0:T(8,128)S(1)} %get-tuple-element.25, pred[256,1024]{0,1:T(8,128)(4,1)S(1)} %broadcast_compare_fusion, ...), kind=kOutput, calls=%fused_computation.8 | convolution fusion | flops 564125696 | bytes 34643968 | tf_op jit(solution)/shard_map/rgd,kd->grk/dot_general | solution.py:57
  89.4 7.6 %fusion.2 = (f32[8,256]{1,0:T(8,128)S(1)}, f32[8,256]{1,0:T(8,128)S(1)}, f32[8,256]{1,0:T(8,128)S(1)}) fusion(f32[1024,256,8]{1,0,2:T(8,128)} %get-tuple-element.27, f32[8,256]{1,0:T(8,128)S(1)} %get-tuple-element.3, pred[256,1024]{0,1:T(8,128)(4,1)S(1)} %broadcast_compare_fusion, f32[8,256]{1,0:T(8,128)S(1)} %get-tuple-element.4, ...), kind=kLoop, calls=%fused_computation.10 | loop fusion | flops 25159680 | bytes 25477120 | tf_op jit(solution)/shard_map/reduce_sum | solution.py:62
  97.1 0.0 collective-permute-done.2
  97.1 0.0 collective-permute-done.1
  97.1 1.2 pad_maximum_fusion.1
  98.3 2.3 %divide_convert_fusion = bf16[256,8,128]{0,2,1:T(8,128)(2,1)S(1)} fusion(f32[1024,256,8]{1,0,2:T(8,128)S(1)} %fusion.44, f32[8,256]{1,0:T(8,128)S(1)} %get-tuple-element.5, pred[256,1024]{0,1:T(8,128)(4,1)S(1)} %broadcast_compare_fusion, f32[256,8]{0,1:T(8,128)S(1)} %bitcast.130, bf16[1024,512]{0,1:T(8,128)(2,1)S(1)} %pad_maximum_fusion.1), kind=kOutput, calls=%fused_computation.34 | convolution fusion | flops 545783808 | bytes 9453568 | tf_op jit(solution)/shard_map/grk,kd->rgd/dot_general | solution.py:64
  100.5 0.2 copy.35
  100.8 5.6 %divide_convert_fusion.1 = bf16[256,8,128]{0,2,1:T(8,128)(2,1)S(1)} fusion(f32[1024,256,8]{1,0,2:T(8,128)} %copy-done, f32[8,256]{1,0:T(8,128)S(1)} %get-tuple-element.4, pred[256,1024]{0,1:T(8,128)(4,1)S(1)} %broadcast_compare_fusion, f32[256,8]{0,1:T(8,128)S(1)} %bitcast.129, bf16[1024,512]{0,1:T(8,128)(2,1)S(1)} %pad_maximum_fusion.1), kind=kOutput, calls=%fused_computation.35 | convolution fusion | flops 545783808 | bytes 9453568 | tf_op jit(solution)/shard_map/grk,kd->rgd/dot_general | solution.py:64
  106.3 0.2 copy.34
  106.5 5.6 %divide_convert_fusion.2 = bf16[256,8,128]{0,2,1:T(8,128)(2,1)S(1)} fusion(f32[1024,256,8]{1,0,2:T(8,128)} %get-tuple-element.27, f32[8,256]{1,0:T(8,128)S(1)} %get-tuple-element.3, pred[256,1024]{0,1:T(8,128)(4,1)S(1)} %broadcast_compare_fusion, f32[256,8]{0,1:T(8,128)S(1)} %bitcast.128, bf16[1024,512]{0,1:T(8,128)(2,1)S(1)} %pad_maximum_fusion.1), kind=kOutput, calls=%fused_computation.36 | convolution fusion | flops 545783808 | bytes 9453568 | tf_op jit(solution)/shard_map/grk,kd->rgd/dot_general | solution.py:64
  112.1 0.2 copy.33
  112.3 5.6 %divide_convert_fusion.3 = bf16[256,8,128]{0,2,1:T(8,128)(2,1)S(1)} fusion(f32[1024,256,8]{1,0,2:T(8,128)} %get-tuple-element.26, f32[8,256]{1,0:T(8,128)S(1)} %get-tuple-element.25, pred[256,1024]{0,1:T(8,128)(4,1)S(1)} %broadcast_compare_fusion, f32[256,8]{0,1:T(8,128)S(1)} %bitcast.131, bf16[1024,512]{0,1:T(8,128)(2,1)S(1)} %pad_maximum_fusion.1), kind=kOutput, calls=%fused_computation.37 | convolution fusion | flops 545783808 | bytes 9453568 | tf_op jit(solution)/shard_map/grk,kd->rgd/dot_general | solution.py:64
  117.9 0.2 copy.32
  118.1 1.5 %pad_maximum_fusion = bf16[256,4096]{1,0:T(8,128)(2,1)} fusion(bf16[256,1024]{1,0:T(8,128)(2,1)S(1)} %copy.35, bf16[256,1024]{1,0:T(8,128)(2,1)S(1)} %copy.34, bf16[256,1024]{1,0:T(8,128)(2,1)S(1)} %copy.33, bf16[256,1024]{1,0:T(8,128)(2,1)S(1)} %copy.32), kind=kLoop, calls=%fused_computation.28 | loop fusion | flops 8388608 | bytes 4194304 | tf_op jit(solution)/shard_map/concatenate | solution.py:68
  119.6 0.6 pad_maximum_fusion.2
  (9 shorter events, 0.0 us)
Async XLA Ops:
  0.6 32.2 %collective-permute-start.3 = (bf16[256,512]{1,0:T(8,128)(2,1)}, bf16[256,512]{1,0:T(8,128)(2,1)}, u32[]{:S(2)}, u32[]{:S(2)}) collective-permute-start(bf16[256,512]{1,0:T(8,128)(2,1)} %param.5), channel_id=1, source_target_pairs={{480,0},{0,32},{32,64},{64,96},{96,128},{128,160},{160,192},{192,2... | collective-permute-start | bytes 786440 | tf_op jit(solution)/shard_map/ppermute | solution.py:13
  9.7 60.6 %collective-permute-start.5 = (bf16[256,512]{1,0:T(8,128)(2,1)}, bf16[256,512]{1,0:T(8,128)(2,1)S(1)}, u32[]{:S(2)}, u32[]{:S(2)}) collective-permute-start(bf16[256,512]{1,0:T(8,128)(2,1)} %param.5), channel_id=1, source_target_pairs={{31,0},{0,1},{1,2},{2,3},{3,4},{4,5},{5,6},{6,7},{7,8},{8,9},{9,10... | collective-permute-start | bytes 786440 | tf_op jit(solution)/shard_map/ppermute | solution.py:13
  13.4 83.6 %collective-permute-start.2 = (bf16[256,512]{0,1:T(8,128)(2,1)S(1)}, bf16[256,512]{0,1:T(8,128)(2,1)}, u32[]{:S(2)}, u32[]{:S(2)}) collective-permute-start(bf16[256,512]{0,1:T(8,128)(2,1)S(1)} %copy.19), channel_id=1, source_target_pairs={{31,0},{0,1},{1,2},{2,3},{3,4},{4,5},{5,6},{6,7},{7,8},{8,9},{9,10... | collective-permute-start | bytes 786440 | tf_op jit(solution)/shard_map/ppermute | solution.py:13
  20.9 30.4 %collective-permute-start = (bf16[256,512]{0,1:T(8,128)(2,1)S(1)}, bf16[256,512]{0,1:T(8,128)(2,1)}, u32[]{:S(2)}, u32[]{:S(2)}) collective-permute-start(bf16[256,512]{0,1:T(8,128)(2,1)S(1)} %copy.19), channel_id=1, source_target_pairs={{480,0},{0,32},{32,64},{64,96},{96,128},{128,160},{160,192},{192,2... | collective-permute-start | bytes 786440 | tf_op jit(solution)/shard_map/ppermute | solution.py:13
  32.8 35.8 %collective-permute-start.4 = (bf16[256,512]{1,0:T(8,128)(2,1)}, bf16[256,512]{1,0:T(8,128)(2,1)}, u32[]{:S(2)}, u32[]{:S(2)}) collective-permute-start(bf16[256,512]{1,0:T(8,128)(2,1)} %collective-permute-done.3), channel_id=1, source_target_pairs={{480,0},{0,32},{32,64},{64,96},{96,128},{128,160},{160,192},{192,2... | collective-permute-start | bytes 786440 | tf_op jit(solution)/shard_map/ppermute | solution.py:13
  51.3 45.7 %collective-permute-start.1 = (bf16[256,512]{0,1:T(8,128)(2,1)}, bf16[256,512]{0,1:T(8,128)(2,1)S(1)}, u32[]{:S(2)}, u32[]{:S(2)}) collective-permute-start(bf16[256,512]{0,1:T(8,128)(2,1)} %collective-permute-done), channel_id=1, source_target_pairs={{480,0},{0,32},{32,64},{64,96},{96,128},{128,160},{160,192},{192,2... | collective-permute-start | bytes 786440 | tf_op jit(solution)/shard_map/ppermute | solution.py:13
  71.0 2.3 %copy-start.1 = (bf16[1024,512]{1,0:T(8,128)(2,1)S(1)}, bf16[1024,512]{1,0:T(8,128)(2,1)}, u32[]{:S(2)}) copy-start(bf16[1024,512]{1,0:T(8,128)(2,1)} %constant_dynamic-update-slice_fusion) | copy-start | bytes 3145732
  73.3 6.2 %copy-start.2 = (bf16[256,1024]{0,1:T(8,128)(2,1)S(1)}, bf16[256,1024]{0,1:T(8,128)(2,1)}, u32[]{:S(2)}) copy-start(bf16[256,1024]{0,1:T(8,128)(2,1)} %copy.45) | copy-start | bytes 1572868
  74.5 14.8 %copy-start = (f32[1024,256,8]{1,0,2:T(8,128)}, f32[1024,256,8]{1,0,2:T(8,128)S(1)}, u32[]{:S(2)}) copy-start(f32[1024,256,8]{1,0,2:T(8,128)S(1)} %fusion.45) | copy-start | bytes 25165828
where the time goes:
time: 121 us; the launch traced here: 120 us
  starting transfers between devices  43.3 us (36%)
  matrix products  37.3 us (31%)
  other arithmetic  16.2 us (13%)
  local copies, waits for them, and re-layouts  13.6 us (11%)
  waiting for transfers between devices  8.9 us (7%)
    ppermute x6, starting transfers between devices, passed_along(): return lax.ppermute(block, axis, route)  43.3 us
    dot_general x4, matrix products, local(): jnp.einsum('grk,kd->rgd', weights, head_v, preferred_element_type=jnp.flo...  18.9 us
    dot_general x4, matrix products, local(): jnp.einsum('rgd,kd->grk', head_q, head_k, preferred_element_type=jnp.floa...  18.3 us
    ppermute x6, waiting for transfers between devices, passed_along(): return lax.ppermute(block, axis, route)  8.9 us
    unnamed x14, local copies, waits for them, and re-layouts  7.72 us
    reduce_sum x1, other arithmetic, local(): total = jnp.sum(expo, axis=-1)  7.65 us
    add x3, other arithmetic, block_positions(): return first * half_rows + offsets % half_rows  5 us
  transfers between devices with their start and end apart: 6, of which 1 were waited for; matrix products, arithmetic and copies ran while one was open for 37% of the time, Pallas kernels for 0%

commit v1 on v0

v1 whole, which is shorter than its diff:
```python
import functools
import math

import jax
import jax.numpy as jnp
from jax import lax
from jax.experimental import pallas as pl
from jax.experimental.pallas import tpu as pltpu
from jax.sharding import PartitionSpec as P

D = 128
T = 128
GROUP = 8
CHUNK = 4
LOG2E = math.log2(math.e)
SCALE = D**-0.5 * LOG2E
AXES = ("inner", "outer")
Y = 4
CORES = 2


def attend(q, k_ref, v_ref, first, n, masks):
    scores = lax.dot_general(
        q, k_ref[first * T : (first + n) * T, :], (((1,), (1,)), ((), ())), preferred_element_type=jnp.float32
    )
    parts = [scores[:, i * T : (i + 1) * T] for i in range(n)]
    for i, mask in masks.items():
        parts[i] = jnp.where(mask, parts[i], -jnp.inf)
    top = jnp.max(functools.reduce(jnp.maximum, parts), axis=1, keepdims=True) * SCALE
    weights = jnp.concatenate([jnp.exp2(x * SCALE - top).astype(jnp.bfloat16) for x in parts], axis=1)
    summed = lax.dot_general(
        weights, v_ref[first * T : (first + n) * T, :], (((1,), (0,)), ((), ())), preferred_element_type=jnp.float32
    )
    return summed[:, :D], summed[:, D:], top


def attention_body(
    half, meta, spans, q_ref, k_ref, v_ref, near_a, near_b, far_a, far_b, far_c, side_ref, *rest
):
    out_ref, log_ref, k_all, v_all, tops, totals = rest[-6:]
    kv = pl.program_id(0)

    def place(i):
        a = spans[meta[i]]
        flip = a >= 512
        low = pl.multiple_of(jnp.where(flip, T, 0), T)
        high = pl.multiple_of(jnp.where(flip, 0, T), T)
        return jnp.where(flip, 1023 - a, a), low, high

    at_start, at_even = meta[4] == 1, meta[5] == 1
    own, low_at, high_at = place(0)
    blocks = [place(i) for i in range(1, 4)]
    lows = [b[0] < own for b in blocks]
    n_low = sum(x.astype(jnp.int32) for x in lows)
    k_cols = pl.ds(pl.multiple_of(kv * D, D), D)
    v_cols = pl.ds(pl.multiple_of((2 + kv) * D, D), D)
    ones = jnp.ones((T, D), jnp.bfloat16)
    none = jnp.zeros((T, D), jnp.bfloat16)

    def put(slot, k, v, one):
        rows = pl.ds(pl.multiple_of(slot * T, T), T)
        k_all[rows, :] = k
        v_all[rows, :D] = v
        v_all[rows, D:] = one

    def near(rows, cols):
        return jnp.where(at_start & at_even, near_b[rows, cols], near_a[rows, cols])

    def far(rows, cols):
        crossed = far_b[rows, cols] if far_c is None else jnp.where(at_even, far_b[rows, cols], far_c[rows, cols])
        return jnp.where(at_start, crossed, far_a[rows, cols])

    def side(rows, cols):
        return side_ref[rows, cols]

    low_rows, high_rows = pl.ds(low_at, T), pl.ds(high_at, T)
    put(0, k_ref[low_rows, :], v_ref[low_rows, :], ones)
    put(4, k_ref[high_rows, :], v_ref[high_rows, :], ones)
    put(5, k_ref[low_rows, :], v_ref[low_rows, :], ones)
    rank = jnp.int32(0)
    for i, read in enumerate((near, far, side)):
        _, block_low, block_high = blocks[i]
        rows = pl.ds(block_low, T)
        put(6 + i, read(rows, k_cols), read(rows, v_cols), ones)
        rows = pl.ds(pl.multiple_of(jnp.where(lows[i], block_low, block_high), T), T)
        put(jnp.where(lows[i], 1 + rank, 9 + i - rank), read(rows, k_cols), read(rows, v_cols), ones)
        rank = rank + lows[i].astype(jnp.int32)
    many = n_low >= 2
    spare = jnp.where(many, jnp.where(n_low == 2, 3, 9), jnp.where(n_low == 0, 1, 11))
    put(spare, jnp.where(n_low == 2, k_all[T : 2 * T, :], k_ref[low_rows, :]), none, none)

    row = lax.broadcasted_iota(jnp.int32, (CHUNK * T, T), 0) % T
    col = lax.broadcasted_iota(jnp.int32, (CHUNK * T, T), 1)
    lane = lax.broadcasted_iota(jnp.int32, (T, T), 1)

    def chunk_of_heads(g, low_tiles):
        cols = [pl.ds(pl.multiple_of((g * CHUNK + j) * D, D), D) for j in range(CHUNK)]

        def queries(rows):
            return jnp.concatenate([q_ref[rows, c] for c in cols], axis=0)

        masks = {0: col <= row}
        if low_tiles == 2:
            low_masks = {0: col <= row, 1: col <= jnp.where(n_low == 0, row, T)}
        else:
            low_masks = masks
        results = (
            attend(queries(low_rows), k_all, v_all, 0, low_tiles, low_masks),
            attend(queries(high_rows), k_all, v_all, 4, 10 - low_tiles, masks),
        )
        for w, (rows, (summed, total, top)) in enumerate(zip((low_rows, high_rows), results)):
            result = (summed / total).astype(out_ref.dtype)
            for j in range(CHUNK):
                part = slice(j * T, (j + 1) * T)
                out_ref[rows, cols[j]] = result[part]
                here = lane == kv * GROUP + g * CHUNK + j
                tops[w] = jnp.where(here, top[part], tops[w])
                totals[w] = jnp.where(here, total[part], totals[w])

    for low_tiles in (2, 4):

        @pl.when(many == (low_tiles == 4))
        def _():
            def step(g, carry):
                chunk_of_heads(g, low_tiles)
                return carry

            lax.fori_loop(0, GROUP // CHUNK, step, 0, unroll=True)

    @pl.when(kv == 1)
    def _():
        for w, at in enumerate((low_at, high_at)):
            log_sum = (tops[w] + jnp.log2(totals[w])) * (1.0 / LOG2E)
            log_ref[:, pl.ds(at, T)] = jnp.transpose(log_sum)[: 2 * GROUP]


def attention(half, meta, spans, q, k, v, near, far, side, filled=None):
    rows = q.shape[0]
    piece = (rows, 4 * D)

    def heads(i):
        return (0, 2 * half + i)

    def block(array):
        at = half if array.shape[0] > rows else 0
        return pl.BlockSpec(piece, lambda i: (at, 0))

    smem = pl.BlockSpec(memory_space=pltpu.SMEM)
    arrays = [*near, *far, side]
    in_specs = [
        smem,
        smem,
        pl.BlockSpec((rows, GROUP * D), heads),
        pl.BlockSpec((rows, D), heads),
        pl.BlockSpec((rows, D), heads),
    ] + [block(a) for a in arrays]
    args = [meta, spans, q, k, v, *arrays]
    alias = {}
    if filled is not None:
        alias = {len(args): 0, len(args) + 1: 1}
        in_specs += [pl.BlockSpec(memory_space=pl.ANY)] * 2
        args += filled

    def body(*refs):
        refs = list(refs)
        if len(far) == 2:
            refs.insert(9, None)
        attention_body(half, *refs)

    q_heads = q.shape[1] // D
    return pl.pallas_call(
        body,
        grid=(2,),
        out_shape=(
            jax.ShapeDtypeStruct(q.shape, jnp.bfloat16),
            jax.ShapeDtypeStruct((q_heads, rows), jnp.float32),
        ),
        in_specs=in_specs,
        out_specs=(
            pl.BlockSpec((rows, GROUP * D), heads),
            pl.BlockSpec((2 * GROUP, rows), lambda i: (half, 0)),
        ),
        scratch_shapes=[
            pltpu.VMEM((12 * T, D), jnp.bfloat16),
            pltpu.VMEM((12 * T, 2 * D), jnp.bfloat16),
            pltpu.VMEM((2, T, T), jnp.float32),
            pltpu.VMEM((2, T, T), jnp.float32),
        ],
        input_output_aliases=alias,
        compiler_params=pltpu.CompilerParams(vmem_limit_bytes=40 * 2**20),
        cost_estimate=pl.CostEstimate(flops=2_400_000_000, bytes_accessed=4_000_000, transcendentals=2_400_000),
        name=f"attention_{half}",
    )(*args)


def local(n_inner, n_outer, queries, keys, values, spans):
    n_high = n_inner // (Y * CORES)

    def at(high, y, core, o):
        return ((high % n_high * Y + y % Y) * CORES + core) * n_outer + o % n_outer

    def send(block, *moves):
        route = []
        for move in moves:
            for high in range(n_high):
                for o in range(n_outer):
                    for source, target in move(high):
                        route.append((at(*source, o), at(*target, o)))
        return lax.ppermute(block, AXES, sorted(route))

    inner_at = lax.axis_index("inner")
    outer_at = lax.axis_index("outer")
    y_at = inner_at // CORES % Y
    core_at = inner_at % CORES
    meta = jnp.stack(
        [
            inner_at * n_outer + outer_at,
            (inner_at - 1) % n_inner * n_outer + outer_at,
            (inner_at - 2) % n_inner * n_outer + outer_at,
            inner_at * n_outer + (outer_at - 1) % n_outer,
            (y_at == 0).astype(jnp.int32),
            (core_at == 0).astype(jnp.int32),
        ]
    ).astype(jnp.int32)
    first_spans = spans[:, 0]

    width = 2 * D
    first = jnp.concatenate([keys[:, :width], values[:, :width]], axis=1)
    second = jnp.concatenate([keys[:, width:], values[:, width:]], axis=1)
    whole = jnp.concatenate([first, second], axis=0)

    last = Y - 1
    spread_first = send(first, lambda h: [((h, last, 0), (h, 0, 0)), ((h, last, 1), (h, 1, 1))])
    spread_second = send(second, lambda h: [((h, last, 0), (h + 1, 0, 0)), ((h, last, 1), (h, 2, 1))])
    stepped = send(whole, lambda h: [((h, y, c), (h, y + 1, c)) for y in range(last) for c in range(CORES)])
    side = lax.ppermute(
        whole,
        AXES,
        [(i * n_outer + (o - 1) % n_outer, i * n_outer + o) for i in range(n_inner) for o in range(n_outer)],
    )
    crossed_first = send(spread_first, lambda h: [((h, 0, 0), (h + 1, 0, 0)), ((h, 1, 1), (h + 1, 0, 1))])
    crossed_second = send(spread_second, lambda h: [((h, 2, 1), (h + 1, 0, 1))])
    swapped = send(
        jnp.where(core_at == 0, whole, stepped),
        lambda h: [((h, y, 0), (h, y, 1)) for y in range(Y)] + [((h, y, 1), (h, y, 0)) for y in range(1, Y)],
    )
    handed_first = send(crossed_first, lambda h: [((h, 0, 1), (h, 0, 0))])
    handed_second = send(crossed_second, lambda h: [((h, 0, 1), (h, 0, 0))])

    filled = attention(
        0, meta, first_spans, queries, keys, values, (swapped, handed_first), (stepped, crossed_first), side
    )
    return attention(
        1,
        meta,
        first_spans,
        queries,
        keys,
        values,
        (swapped, handed_second),
        (stepped, spread_second, crossed_second),
        side,
        filled,
    )


def solution(mesh):
    placed = P(AXES, None)
    return jax.shard_map(
        functools.partial(local, mesh.shape["inner"], mesh.shape["outer"]),
        mesh=mesh,
        in_specs=(placed, placed, placed, P()),
        out_specs=(placed, P(None, AXES)),
        check_vma=False,
    )
```

time: 121 us -> 75.4 us (0.62)
  the two profiles are of different devices: /device:TPU:217 before, /device:TPU:33 now
where the time goes in v1:
time: 75.4 us; the launch traced here: 75 us
  waiting for transfers between devices  33.7 us (45%)
  starting transfers between devices  20 us (27%)
  Pallas kernels  14.9 us (20%)
  other arithmetic  4.27 us (6%)
  local copies, waits for them, and re-layouts  1.26 us (2%)
  between operations  0.82 us (1%)
    ppermute x8, waiting for transfers between devices, send(): return lax.ppermute(block, AXES, sorted(route))  33.7 us
    ppermute x8, starting transfers between devices, send(): return lax.ppermute(block, AXES, sorted(route))  16.5 us
    pallas_call x2, Pallas kernels, attention(): pl.pallas_call(body, grid=(2,), out_shape=(jax.ShapeDtypeStruct(q.shape,...  14.9 us
    ppermute x1, starting transfers between devices, local(): lax.ppermute(whole, AXES, [(i * n_outer + (o - 1) % n_outer, i * n_outer...  3.54 us
    select_n x1, other arithmetic, local(): jnp.where(core_at == 0, whole, stepped)  1.96 us
  transfers between devices with their start and end apart: 9, of which 2 were waited for; matrix products, arithmetic and copies ran while one was open for 5% of the time, Pallas kernels for 10%

profile of v1, /device:TPU:33, one launch (start us, length us, event | category | flops | bytes accessed | tf_op | source)
XLA Modules:
  0.0 75.0 jit_solution(12966837606281242656)
XLA Ops:
  0.6 1.1 %fusion = (bf16[256,256]{1,0:T(8,128)(2,1)S(1)}, bf16[256,256]{1,0:T(8,128)(2,1)S(1)}, bf16[256,256]{1,0:T(8,128)(2,1)S(1)}, bf16[256,256]{1,0:T(8,128)(2,1)S(1)}) fusion(bf16[256,512]{1,0:T(8,128)(2,1)} %refs_3_.3, bf16[256,512]{1,0:T(8,128)(2,1)} %refs_4_.3), kind=kLoop, calls=%fused_computation.4 | loop fusion | bytes 1048576 | tf_op jit(solution)/shard_map/slice | solution.py:228
  1.8 0.0 copy-start.3
  1.8 0.0 copy-start.4
  1.8 0.0 copy-start.5
  1.8 0.0 copy-start.6
  1.8 0.0 copy-start
  1.8 0.0 copy-start.1
  1.8 0.0 copy-start.2
  1.8 0.8 %maximum_maximum_fusion = bf16[512,512]{1,0:T(8,128)(2,1)} fusion(bf16[256,256]{1,0:T(8,128)(2,1)S(1)} %get-tuple-element.10, bf16[256,256]{1,0:T(8,128)(2,1)S(1)} %get-tuple-element.7, bf16[256,256]{1,0:T(8,128)(2,1)S(1)} %get-tuple-element.11, bf16[256,256]{1,0:T(8,128)(2,1)S(1)} %get-tuple-element.6), kind=kLoop, calls=%fused_computation | loop fusion | flops 2097152 | bytes 1048576 | tf_op jit(solution)/shard_map/concatenate | solution.py:230
  2.7 3.4 %collective-permute-start = (bf16[512,512]{1,0:T(8,128)(2,1)}, bf16[512,512]{1,0:T(8,128)(2,1)S(1)}, u32[]{:S(2)}, u32[]{:S(2)}) collective-permute-start(bf16[512,512]{1,0:T(8,128)(2,1)} %maximum_maximum_fusion), channel_id=1, source_target_pairs={{0,64},{1,65},{2,66},{3,67},{4,68},{5,69},{6,70},{7,71},{8,72},{9,... | collective-permute-start | bytes 1572872 | tf_op jit(solution)/shard_map/ppermute | solution.py:209
  6.0 0.7 pad_maximum_fusion
  6.8 1.4 %collective-permute-start.6 = (bf16[256,512]{1,0:T(8,128)(2,1)}, bf16[256,512]{1,0:T(8,128)(2,1)}, u32[]{:S(2)}, u32[]{:S(2)}) collective-permute-start(bf16[256,512]{1,0:T(8,128)(2,1)} %pad_maximum_fusion), channel_id=1, source_target_pairs={{192,0},{193,1},{194,2},{195,3},{196,4},{197,5},{198,6},{199,7},{2... | collective-permute-start | bytes 786440 | tf_op jit(solution)/shard_map/ppermute | solution.py:209
  8.1 3.5 %collective-permute-start.5 = (bf16[512,512]{1,0:T(8,128)(2,1)}, bf16[512,512]{1,0:T(8,128)(2,1)}, u32[]{:S(2)}, u32[]{:S(2)}) collective-permute-start(bf16[512,512]{1,0:T(8,128)(2,1)} %maximum_maximum_fusion), channel_id=1, source_target_pairs={{31,0},{0,1},{1,2},{2,3},{3,4},{4,5},{5,6},{6,7},{7,8},{8,9},{9,10... | collective-permute-start | bytes 1572872 | tf_op jit(solution)/shard_map/ppermute | solution.py:236
  11.7 0.0 copy-done.3
  11.7 0.0 copy-done.4
  11.7 0.8 %pad_maximum_fusion.1 = bf16[256,512]{1,0:T(8,128)(2,1)} fusion(bf16[256,256]{1,0:T(8,128)(2,1)S(1)} %get-tuple-element.10, bf16[256,256]{1,0:T(8,128)(2,1)S(1)} %get-tuple-element.7), kind=kLoop, calls=%fused_computation.3 | loop fusion | flops 524288 | bytes 524288 | tf_op jit(solution)/shard_map/concatenate | solution.py:229
  12.4 0.0 copy-done.5
  12.4 0.7 collective-permute-start.2
  13.1 0.0 collective-permute-done.6
  13.1 1.3 %collective-permute-start.7 = (bf16[256,512]{1,0:T(8,128)(2,1)}, bf16[256,512]{1,0:T(8,128)(2,1)}, u32[]{:S(2)}, u32[]{:S(2)}) collective-permute-start(bf16[256,512]{1,0:T(8,128)(2,1)} %collective-permute-done.6), channel_id=1, source_target_pairs={{0,256},{1,257},{2,258},{3,259},{4,260},{5,261},{6,262},{7,263},{8... | collective-permute-start | bytes 786440 | tf_op jit(solution)/shard_map/ppermute | solution.py:209
  14.4 2.4 %collective-permute-done.refs_7_ = bf16[512,512]{1,0:T(8,128)(2,1)S(1)} collective-permute-done((bf16[512,512]{1,0:T(8,128)(2,1)}, bf16[512,512]{1,0:T(8,128)(2,1)S(1)}, u32[]{:S(2)}, u32[]{:S(2)}) %collective-permute-start) | collective-permute-done | bytes 524320 | tf_op jit(solution)/shard_map/ppermute | solution.py:209
  16.9 2.0 %broadcast_select_fusion = bf16[512,512]{1,0:T(8,128)(2,1)} fusion(bf16[512,512]{1,0:T(8,128)(2,1)S(1)} %collective-permute-done.refs_7_, pred[]{:T(512)S(6)} %eq.14, bf16[256,256]{1,0:T(8,128)(2,1)} %copy-done.4, bf16[256,256]{1,0:T(8,128)(2,1)} %copy-done.3, bf16[256,256]{1,0:T(8,128)(2,1)} %copy-done.5, bf16[256,256]{1,0:T(8,128)(2,1)S(1)} %get-tuple-element.6), kind=kLoop, calls=%fused_computation.1 | loop fusion | flops 2359296 | bytes 1572865 | tf_op jit(solution)/shard_map/jit(_where)/select_n | solution.py:244
  18.9 1.3 %collective-permute-start.1 = (bf16[512,512]{1,0:T(8,128)(2,1)}, bf16[512,512]{1,0:T(8,128)(2,1)}, u32[]{:S(2)}, u32[]{:S(2)}) collective-permute-start(bf16[512,512]{1,0:T(8,128)(2,1)} %broadcast_select_fusion), channel_id=1, source_target_pairs={{0,32},{1,33},{2,34},{3,35},{4,36},{5,37},{6,38},{7,39},{8,40},{9,... | collective-permute-start | bytes 1572872 | tf_op jit(solution)/shard_map/ppermute | solution.py:209
  20.1 0.0 collective-permute-done.2.refs_8_
  20.2 1.3 %collective-permute-start.3 = (bf16[256,512]{1,0:T(8,128)(2,1)S(1)}, bf16[256,512]{1,0:T(8,128)(2,1)}, u32[]{:S(2)}, u32[]{:S(2)}) collective-permute-start(bf16[256,512]{1,0:T(8,128)(2,1)S(1)} %collective-permute-done.2.refs_8_), channel_id=1, source_target_pairs={{160,288},{161,289},{162,290},{163,291},{164,292},{165,293},{166,2... | collective-permute-start | bytes 786440 | tf_op jit(solution)/shard_map/ppermute | solution.py:209
  21.5 31.3 %collective-permute-done.7.refs_8_ = bf16[256,512]{1,0:T(8,128)(2,1)} collective-permute-done((bf16[256,512]{1,0:T(8,128)(2,1)}, bf16[256,512]{1,0:T(8,128)(2,1)}, u32[]{:S(2)}, u32[]{:S(2)}) %collective-permute-start.7) | collective-permute-done | bytes 262176 | tf_op jit(solution)/shard_map/ppermute | solution.py:209
  52.7 5.2 %collective-permute-start.8 = (bf16[256,512]{1,0:T(8,128)(2,1)}, bf16[256,512]{1,0:T(8,128)(2,1)}, u32[]{:S(2)}, u32[]{:S(2)}) collective-permute-start(bf16[256,512]{1,0:T(8,128)(2,1)} %collective-permute-done.7.refs_8_), channel_id=1, source_target_pairs={{32,0},{33,1},{34,2},{35,3},{36,4},{37,5},{38,6},{39,7},{40,8},{41... | collective-permute-start | bytes 786440 | tf_op jit(solution)/shard_map/ppermute | solution.py:209
  57.9 0.0 collective-permute-done.3.refs_9_
  57.9 2.0 %collective-permute-start.4 = (bf16[256,512]{1,0:T(8,128)(2,1)}, bf16[256,512]{1,0:T(8,128)(2,1)}, u32[]{:S(2)}, u32[]{:S(2)}) collective-permute-start(bf16[256,512]{1,0:T(8,128)(2,1)} %collective-permute-done.3.refs_9_), channel_id=1, source_target_pairs={{32,0},{33,1},{34,2},{35,3},{36,4},{37,5},{38,6},{39,7},{40,8},{41... | collective-permute-start | bytes 786440 | tf_op jit(solution)/shard_map/ppermute | solution.py:209
  59.9 0.0 copy-done.6
  59.9 0.1 stack.35.refs_0_
  60.0 0.0 collective-permute-done.5.refs_9_.refs_10_
  60.0 0.0 collective-permute-done.8.refs_6_
  60.0 0.0 collective-permute-done.1.refs_5_
  60.0 0.0 copy-done
  60.1 0.0 copy-done.1
  60.1 0.0 copy-done.2
  60.1 7.5 %attention_0.1 = (bf16[256,4096]{1,0:T(8,128)(2,1)}, f32[32,256]{1,0:T(8,128)}) custom-call(s32[6]{0:T(128)S(1)} %stack.35.refs_0_, s32[512]{0:T(512)S(1)} %bitcast.7, bf16[256,4096]{1,0:T(8,128)(2,1)S(1)} %copy-done.2, bf16[256,512]{1,0:T(8,128)(2,1)S(1)} %copy-done, bf16[256,512]{1,0:T(8,128)(2,1)S(1)} %copy-done.1, ...), custom_call_target="tpu_custom_call" | custom-call | flops 2400000000 | bytes 4000000 | tf_op jit(solution)/shard_map/attention_0/pallas_call | solution.py:171
  67.5 0.0 collective-permute-done.4.refs_6_
  67.5 7.5 %attention_1.1 = (bf16[256,4096]{1,0:T(8,128)(2,1)}, f32[32,256]{1,0:T(8,128)}) custom-call(s32[6]{0:T(128)S(1)} %stack.35.refs_0_, s32[512]{0:T(512)S(1)} %bitcast.8, bf16[256,4096]{1,0:T(8,128)(2,1)S(1)} %copy-done.2, bf16[256,512]{1,0:T(8,128)(2,1)S(1)} %copy-done, ...), custom_call_target="tpu_custom_call", output_to_operand_aliasing={{0}: (11, {}), {1}: (12, {})} | custom-call | flops 2400000000 | bytes 4000000 | tf_op jit(solution)/shard_map/attention_1/pallas_call | solution.py:171
  (1 shorter events, 0.0 us)
Async XLA Ops:
  1.8 9.9 %copy-start.3 = (bf16[256,256]{1,0:T(8,128)(2,1)}, bf16[256,256]{1,0:T(8,128)(2,1)S(1)}, u32[]{:S(2)}) copy-start(bf16[256,256]{1,0:T(8,128)(2,1)S(1)} %get-tuple-element.7) | copy-start | bytes 393220
  1.8 9.9 %copy-start.4 = (bf16[256,256]{1,0:T(8,128)(2,1)}, bf16[256,256]{1,0:T(8,128)(2,1)S(1)}, u32[]{:S(2)}) copy-start(bf16[256,256]{1,0:T(8,128)(2,1)S(1)} %get-tuple-element.10) | copy-start | bytes 393220
  1.8 10.7 %copy-start.5 = (bf16[256,256]{1,0:T(8,128)(2,1)}, bf16[256,256]{1,0:T(8,128)(2,1)S(1)}, u32[]{:S(2)}) copy-start(bf16[256,256]{1,0:T(8,128)(2,1)S(1)} %get-tuple-element.11) | copy-start | bytes 393220
  1.8 58.1 %copy-start.6 = (s32[512,2]{0,1:T(2,128)S(1)}, s32[512,2]{0,1:T(2,128)}, u32[]{:S(2)}) copy-start(s32[512,2]{0,1:T(2,128)} %param.7) | copy-start | bytes 12292
  1.8 58.2 %copy-start = (bf16[256,512]{1,0:T(8,128)(2,1)S(1)}, bf16[256,512]{1,0:T(8,128)(2,1)}, u32[]{:S(2)}) copy-start(bf16[256,512]{1,0:T(8,128)(2,1)} %refs_3_.3) | copy-start | bytes 786436
  1.8 58.2 %copy-start.1 = (bf16[256,512]{1,0:T(8,128)(2,1)S(1)}, bf16[256,512]{1,0:T(8,128)(2,1)}, u32[]{:S(2)}) copy-start(bf16[256,512]{1,0:T(8,128)(2,1)} %refs_4_.3) | copy-start | bytes 786436
  1.8 58.2 %copy-start.2 = (bf16[256,4096]{1,0:T(8,128)(2,1)S(1)}, bf16[256,4096]{1,0:T(8,128)(2,1)}, u32[]{:S(2)}) copy-start(bf16[256,4096]{1,0:T(8,128)(2,1)} %refs_2_.3) | copy-start | bytes 6291460
  2.7 14.2 %collective-permute-start = (bf16[512,512]{1,0:T(8,128)(2,1)}, bf16[512,512]{1,0:T(8,128)(2,1)S(1)}, u32[]{:S(2)}, u32[]{:S(2)}) collective-permute-start(bf16[512,512]{1,0:T(8,128)(2,1)} %maximum_maximum_fusion), channel_id=1, source_target_pairs={{0,64},{1,65},{2,66},{3,67},{4,68},{5,69},{6,70},{7,71},{8,72},{9,... | collective-permute-start | bytes 1572872 | tf_op jit(solution)/shard_map/ppermute | solution.py:209
  6.8 6.4 %collective-permute-start.6 = (bf16[256,512]{1,0:T(8,128)(2,1)}, bf16[256,512]{1,0:T(8,128)(2,1)}, u32[]{:S(2)}, u32[]{:S(2)}) collective-permute-start(bf16[256,512]{1,0:T(8,128)(2,1)} %pad_maximum_fusion), channel_id=1, source_target_pairs={{192,0},{193,1},{194,2},{195,3},{196,4},{197,5},{198,6},{199,7},{2... | collective-permute-start | bytes 786440 | tf_op jit(solution)/shard_map/ppermute | solution.py:209
  8.1 51.9 %collective-permute-start.5 = (bf16[512,512]{1,0:T(8,128)(2,1)}, bf16[512,512]{1,0:T(8,128)(2,1)}, u32[]{:S(2)}, u32[]{:S(2)}) collective-permute-start(bf16[512,512]{1,0:T(8,128)(2,1)} %maximum_maximum_fusion), channel_id=1, source_target_pairs={{31,0},{0,1},{1,2},{2,3},{3,4},{4,5},{5,6},{6,7},{7,8},{8,9},{9,10... | collective-permute-start | bytes 1572872 | tf_op jit(solution)/shard_map/ppermute | solution.py:236
  12.4 7.7 %collective-permute-start.2 = (bf16[256,512]{1,0:T(8,128)(2,1)}, bf16[256,512]{1,0:T(8,128)(2,1)S(1)}, u32[]{:S(2)}, u32[]{:S(2)}) collective-permute-start(bf16[256,512]{1,0:T(8,128)(2,1)} %pad_maximum_fusion.1), channel_id=1, source_target_pairs={{192,256},{193,257},{194,258},{195,259},{196,260},{197,261},{198,2... | collective-permute-start | bytes 786440 | tf_op jit(solution)/shard_map/ppermute | solution.py:209
  13.1 39.6 %collective-permute-start.7 = (bf16[256,512]{1,0:T(8,128)(2,1)}, bf16[256,512]{1,0:T(8,128)(2,1)}, u32[]{:S(2)}, u32[]{:S(2)}) collective-permute-start(bf16[256,512]{1,0:T(8,128)(2,1)} %collective-permute-done.6), channel_id=1, source_target_pairs={{0,256},{1,257},{2,258},{3,259},{4,260},{5,261},{6,262},{7,263},{8... | collective-permute-start | bytes 786440 | tf_op jit(solution)/shard_map/ppermute | solution.py:209
  18.9 41.2 %collective-permute-start.1 = (bf16[512,512]{1,0:T(8,128)(2,1)}, bf16[512,512]{1,0:T(8,128)(2,1)}, u32[]{:S(2)}, u32[]{:S(2)}) collective-permute-start(bf16[512,512]{1,0:T(8,128)(2,1)} %broadcast_select_fusion), channel_id=1, source_target_pairs={{0,32},{1,33},{2,34},{3,35},{4,36},{5,37},{6,38},{7,39},{8,40},{9,... | collective-permute-start | bytes 1572872 | tf_op jit(solution)/shard_map/ppermute | solution.py:209
  20.2 37.8 %collective-permute-start.3 = (bf16[256,512]{1,0:T(8,128)(2,1)S(1)}, bf16[256,512]{1,0:T(8,128)(2,1)}, u32[]{:S(2)}, u32[]{:S(2)}) collective-permute-start(bf16[256,512]{1,0:T(8,128)(2,1)S(1)} %collective-permute-done.2.refs_8_), channel_id=1, source_target_pairs={{160,288},{161,289},{162,290},{163,291},{164,292},{165,293},{166,2... | collective-permute-start | bytes 786440 | tf_op jit(solution)/shard_map/ppermute | solution.py:209
  52.7 7.3 %collective-permute-start.8 = (bf16[256,512]{1,0:T(8,128)(2,1)}, bf16[256,512]{1,0:T(8,128)(2,1)}, u32[]{:S(2)}, u32[]{:S(2)}) collective-permute-start(bf16[256,512]{1,0:T(8,128)(2,1)} %collective-permute-done.7.refs_8_), channel_id=1, source_target_pairs={{32,0},{33,1},{34,2},{35,3},{36,4},{37,5},{38,6},{39,7},{40,8},{41... | collective-permute-start | bytes 786440 | tf_op jit(solution)/shard_map/ppermute | solution.py:209
  57.9 9.6 %collective-permute-start.4 = (bf16[256,512]{1,0:T(8,128)(2,1)}, bf16[256,512]{1,0:T(8,128)(2,1)}, u32[]{:S(2)}, u32[]{:S(2)}) collective-permute-start(bf16[256,512]{1,0:T(8,128)(2,1)} %collective-permute-done.3.refs_9_), channel_id=1, source_target_pairs={{32,0},{33,1},{34,2},{35,3},{36,4},{37,5},{38,6},{39,7},{40,8},{41... | collective-permute-start | bytes 786440 | tf_op jit(solution)/shard_map/ppermute | solution.py:209

commit v2 on v0

v2 whole, which is shorter than its diff:
```python
import functools
import math

import jax
import jax.numpy as jnp
from jax import lax
from jax.experimental import pallas as pl
from jax.experimental.pallas import tpu as pltpu
from jax.sharding import PartitionSpec as P

D = 128
T = 128
GROUP = 8
CHUNK = 4
LOG2E = math.log2(math.e)
SCALE = D**-0.5 * LOG2E
AXES = ("inner", "outer")
Y = 4
CORES = 2
JOIN = 20_000_000_000


def scores_of(q, k_ref, first, n):
    keys = k_ref[first * T : (first + n) * T, :]
    return lax.dot_general(q, keys, (((1,), (1,)), ((), ())), preferred_element_type=jnp.float32)


def weigh(scores, v_ref, first, n, masks):
    parts = [scores[:, i * T : (i + 1) * T] for i in range(n)]
    for i, mask in masks.items():
        parts[i] = jnp.where(mask, parts[i], -jnp.inf)
    top = jnp.max(functools.reduce(jnp.maximum, parts), axis=1, keepdims=True) * SCALE
    weights = jnp.concatenate([jnp.exp2(x * SCALE - top).astype(jnp.bfloat16) for x in parts], axis=1)
    values = v_ref[first * T : (first + n) * T, :]
    summed = lax.dot_general(weights, values, (((1,), (0,)), ((), ())), preferred_element_type=jnp.float32)
    return top, summed[:, :D], summed[:, D:]


def attention_body(
    meta, spans, q_ref, k_ref, v_ref, handed_k, handed_v, last_k, last_v,
    far_k, far_v, side_k, side_v, out_ref, log_ref, k_all, v_all,
):
    def place(i):
        a = spans[meta[i]]
        flip = a >= 512
        return jnp.where(flip, 1023 - a, a), jnp.where(flip, T, 0), jnp.where(flip, 0, T)

    def rows_at(start):
        return pl.ds(pl.multiple_of(start, T), T)

    at_even = meta[4] == 1

    def near(rows):
        return (
            jnp.where(at_even, last_k[rows, :], handed_k[rows, :]),
            jnp.where(at_even, last_v[rows, :], handed_v[rows, :]),
        )

    def far(rows):
        return far_k[rows, :], far_v[rows, :]

    def side(rows):
        return side_k[rows, :], side_v[rows, :]

    ones = jnp.ones((T, D), v_all.dtype)

    def put(slot, pair, weight=ones):
        rows = rows_at(slot * T)
        k_all[rows, :], v_all[rows, :D] = pair
        v_all[rows, D:] = weight

    own, low_at, high_at = place(0)
    ends = (rows_at(low_at), rows_at(high_at))
    own_low = (k_ref[ends[0], :], v_ref[ends[0], :])
    put(0, own_low)
    put(4, (k_ref[ends[1], :], v_ref[ends[1], :]))
    put(5, own_low)
    n_low = jnp.int32(0)
    for i, read in enumerate((near, far, side)):
        block, block_low, block_high = place(i + 1)
        below = block < own
        put(6 + i, read(rows_at(block_low)))
        put(jnp.where(below, 1 + n_low, 9 + i - n_low), read(rows_at(jnp.where(below, block_low, block_high))))
        n_low = n_low + below.astype(jnp.int32)
    many = n_low >= 2
    spare = jnp.where(many, jnp.where(n_low == 2, 3, 9), jnp.where(n_low == 0, 1, 11))
    none = jnp.zeros((T, D), v_all.dtype)
    put(spare, (jnp.where(n_low == 2, k_all[T : 2 * T, :], own_low[0]), none), none)

    row = lax.broadcasted_iota(jnp.int32, (CHUNK * T, T), 0) % T
    col = lax.broadcasted_iota(jnp.int32, (CHUNK * T, T), 1)
    lane = lax.broadcasted_iota(jnp.int32, (T, T), 1)
    cols = [slice(j * D, (j + 1) * D) for j in range(GROUP)]

    def all_heads(low_tiles):
        first, tiles = (0, 4), (low_tiles, 10 - low_tiles)
        masks = [{0: col <= row}, {0: col <= row}]
        if low_tiles == 2:
            masks[0][1] = col <= jnp.where(n_low == 0, row, T)
        tops, totals = [None, None], [None, None]

        def finish(w, g, scores):
            top, summed, total = weigh(scores, v_all, first[w], tiles[w], masks[w])
            result = (summed * pl.reciprocal(total)).astype(out_ref.dtype)
            for j in range(CHUNK):
                part = slice(j * T, (j + 1) * T)
                out_ref[ends[w], cols[g + j]] = result[part]
                for kept, new in ((tops, top[part]), (totals, total[part])):
                    new = jnp.broadcast_to(new, (T, T))
                    kept[w] = new if kept[w] is None else jnp.where(lane == g + j, new, kept[w])

        waiting = None
        for g in range(0, GROUP, CHUNK):
            for w in (0, 1):
                q = jnp.concatenate([q_ref[ends[w], cols[g + j]] for j in range(CHUNK)], axis=0)
                scores = scores_of(q, k_all, first[w], tiles[w])
                if waiting:
                    finish(*waiting)
                waiting = (w, g, scores)
        finish(*waiting)
        for w in (0, 1):
            log_sum = (tops[w] + jnp.log2(totals[w])) * (1.0 / LOG2E)
            log_ref[:, ends[w]] = jnp.transpose(log_sum)[:GROUP]

    for low_tiles in (2, 4):
        pl.when(many == (low_tiles == 4))(functools.partial(all_heads, low_tiles))


def small_kernel(body, name, flops, outs, *arrays):
    smem = pl.BlockSpec(memory_space=pltpu.SMEM)
    return pl.pallas_call(
        body,
        out_shape=[jax.ShapeDtypeStruct(shape, arrays[-1].dtype) for shape in outs],
        in_specs=[smem if a.ndim == 1 else pl.BlockSpec(a.shape, lambda: (0, 0)) for a in arrays],
        out_specs=[pl.BlockSpec(shape, lambda: (0, 0)) for shape in outs],
        compiler_params=pltpu.CompilerParams(vmem_limit_bytes=16 * 2**20),
        cost_estimate=pl.CostEstimate(flops=flops, bytes_accessed=1_000_000, transcendentals=0),
        name=name,
    )(*arrays)


def pack_body(values, keys, both, relayed, straight, sems):
    rows, cut = values.shape[0], relayed.shape[0]
    copies = [
        (values, relayed.at[:rows]),
        (keys.at[: cut - rows], relayed.at[rows:]),
        (keys.at[cut - rows :], straight),
        (values, both.at[:rows]),
        (keys, both.at[rows:]),
    ]
    copies = [pltpu.make_async_copy(source, to, sems.at[i]) for i, (source, to) in enumerate(copies)]
    for copy in copies:
        copy.start()
    for copy in copies:
        copy.wait()


def pack(values, keys, cut):
    rows, width = keys.shape
    return pl.pallas_call(
        pack_body,
        out_shape=[jax.ShapeDtypeStruct((n, width), keys.dtype) for n in (2 * rows, cut, 2 * rows - cut)],
        in_specs=[pl.BlockSpec(memory_space=pl.ANY)] * 2,
        out_specs=[pl.BlockSpec(memory_space=pltpu.VMEM)] * 3,
        scratch_shapes=[pltpu.SemaphoreType.DMA((5,))],
        compiler_params=pltpu.CompilerParams(vmem_limit_bytes=56 * 2**20),
        name="pack",
    )(values, keys)


def join_body(upper, lower, out):
    rows = upper.shape[0]
    out[:rows, :] = upper[...]
    out[rows:, :] = lower[...]


def choose_body(meta, first, second, out):
    @pl.when(meta[5] == 1)
    def _():
        out[...] = first[...]

    @pl.when(meta[5] == 0)
    def _():
        out[...] = second[...]


def attention(meta, spans, q, *blocks):
    rows, width = q.shape
    smem = pl.BlockSpec(memory_space=pltpu.SMEM)
    vmem = pl.BlockSpec(memory_space=pltpu.VMEM)
    arrays = list({id(array): array for array, _ in blocks}.values())
    where = [([id(a) for a in arrays].index(id(array)), at) for array, at in blocks]

    def body(meta_ref, spans_ref, q_ref, *refs):
        kv = pl.program_id(0)
        columns = pl.ds(pl.multiple_of(kv * D, D), D)
        views = [refs[i].at[at * rows : (at + 1) * rows, columns] for i, at in where]
        q_view = q_ref.at[:, pl.ds(pl.multiple_of(kv * GROUP * D, D), GROUP * D)]
        attention_body(meta_ref, spans_ref, q_view, *views, *refs[len(arrays) :])

    return pl.pallas_call(
        body,
        grid=(width // (GROUP * D),),
        out_shape=(
            jax.ShapeDtypeStruct((rows, width), jnp.bfloat16),
            jax.ShapeDtypeStruct((width // D, rows), jnp.float32),
        ),
        in_specs=[smem, smem, vmem] + [vmem] * len(arrays),
        out_specs=(
            pl.BlockSpec((rows, GROUP * D), lambda i: (0, i)),
            pl.BlockSpec((GROUP, rows), lambda i: (i, 0)),
        ),
        scratch_shapes=[pltpu.VMEM((12 * T, D), jnp.bfloat16), pltpu.VMEM((12 * T, 2 * D), jnp.bfloat16)],
        compiler_params=pltpu.CompilerParams(vmem_limit_bytes=40 * 2**20),
        cost_estimate=pl.CostEstimate(flops=2_400_000_000, bytes_accessed=8_000_000, transcendentals=4_800_000),
        name="attention",
    )(meta, spans, q, *arrays)


def local(n_inner, n_outer, queries, keys, values, spans):
    n_high = n_inner // (Y * CORES)

    def at(high, y, core, o):
        return ((high % n_high * Y + y % Y) * CORES + core) * n_outer + o % n_outer

    def send(block, moves):
        route = [
            (at(*source, o), at(*target, o))
            for high in range(n_high)
            for o in range(n_outer)
            for source, target in moves(high)
        ]
        return lax.ppermute(block, AXES, sorted(route))

    inner_at = lax.axis_index("inner")
    outer_at = lax.axis_index("outer")
    meta = jnp.stack(
        [
            inner_at * n_outer + outer_at,
            (inner_at - 1) % n_inner * n_outer + outer_at,
            (inner_at - 2) % n_inner * n_outer + outer_at,
            inner_at * n_outer + (outer_at - 1) % n_outer,
            (inner_at % CORES == 0).astype(jnp.int32),
            (inner_at // CORES % Y == 0).astype(jnp.int32),
        ]
    ).astype(jnp.int32)
    first_spans = spans[:, 0]
    meta, first_spans = lax.optimization_barrier((meta, first_spans))

    last = Y - 1

    def send_outer(block):
        route = [
            (i * n_outer + o, i * n_outer + (o + 1) % n_outer)
            for i in range(n_inner)
            for o in range(n_outer)
        ]
        return lax.ppermute(block, AXES, route)

    rows, width = keys.shape
    cut = 2 * rows * 9 // 16
    both, relayed, straight = pack(values, keys, cut)
    spread = send(relayed, lambda h: [((h, last, 0), (h, 1, 0)), ((h, last, 1), (h, 2, 1))])
    straight = send(straight, lambda h: [((h, last, c), (h + 1, 0, c)) for c in range(CORES)])
    crossed = send(spread, lambda h: [((h, 1, 0), (h + 1, 0, 0)), ((h, 2, 1), (h + 1, 0, 1))])
    (crossed,) = small_kernel(join_body, "join", JOIN, [(2 * rows, width)], crossed, straight)
    both, spread = lax.optimization_barrier((both, spread))
    side = send_outer(both)
    stepped = send(both, lambda h: [((h, y, c), (h, y + 1, c)) for y in range(last) for c in range(CORES)])
    handed = send(both, lambda h: [((h, y, 0), (h, y, 1)) for y in range(Y)])
    (far,) = small_kernel(choose_body, "choose", 1_000, [(2 * rows, width)], meta, crossed, stepped)
    last_near = send(far, lambda h: [((h, y, 1), (h, y, 0)) for y in range(Y)])
    return attention(
        meta, first_spans, queries, (keys, 0), (values, 0), (handed, 1), (handed, 0), (last_near, 1), (last_near, 0),
        (far, 1), (far, 0), (side, 1), (side, 0),
    )


def solution(mesh):
    placed = P(AXES, None)
    return jax.shard_map(
        lambda *args: tuple(local(mesh.shape["inner"], mesh.shape["outer"], *args)),
        mesh=mesh,
        in_specs=(placed, placed, placed, P()),
        out_specs=(placed, P(None, AXES)),
        check_vma=False,
    )
```

time: 121 us -> 68.8 us (0.57)
  the two profiles are of different devices: /device:TPU:217 before, /device:TPU:39 now
where the time goes in v2:
time: 68.8 us; the launch traced here: 68.5 us
  waiting for transfers between devices  37.4 us (54%)
  starting transfers between devices  16.3 us (24%)
  Pallas kernels  13.2 us (19%)
  between operations  0.83 us (1%)
  local copies, waits for them, and re-layouts  0.79 us (1%)
    ppermute x6, waiting for transfers between devices, send(): return lax.ppermute(block, AXES, sorted(route))  37.4 us
    ppermute x6, starting transfers between devices, send(): return lax.ppermute(block, AXES, sorted(route))  12.5 us
    pallas_call x1, Pallas kernels, attention(): pl.pallas_call(body, grid=(width // (GROUP * D),), out_shape=(jax.ShapeDt...  10.4 us
    ppermute x1, starting transfers between devices, send_outer(): return lax.ppermute(block, AXES, route)  3.81 us
    pallas_call x1, Pallas kernels, pack(): pl.pallas_call(pack_body, out_shape=[jax.ShapeDtypeStruct((n, width), key...  2.25 us
  transfers between devices with their start and end apart: 7, of which 3 were waited for; matrix products, arithmetic and copies ran while one was open for 1% of the time, Pallas kernels for 1%

profile of v2, /device:TPU:39, one launch (start us, length us, event | category | flops | bytes accessed | tf_op | source)
XLA Modules:
  0.0 68.5 jit_solution(2791403431879618809)
XLA Ops:
  0.6 2.2 %pack.1 = (bf16[512,512]{1,0:T(8,128)(2,1)}, bf16[288,512]{1,0:T(8,128)(2,1)}, bf16[224,512]{1,0:T(8,128)(2,1)}) custom-call(bf16[256,512]{1,0:T(8,128)(2,1)} %refs_1_.1, bf16[256,512]{1,0:T(8,128)(2,1)} %refs_0_.1), custom_call_target="tpu_custom_call" | custom-call | tf_op jit(solution)/shard_map/pack/pallas_call | solution.py:160
  2.9 0.7 collective-permute-start
  3.6 0.0 collective-permute-done
  3.6 1.3 %collective-permute-start.2 = (bf16[288,512]{1,0:T(8,128)(2,1)S(1)}, bf16[288,512]{1,0:T(8,128)(2,1)S(1)}, u32[]{:S(2)}, u32[]{:S(2)}) collective-permute-start(bf16[288,512]{1,0:T(8,128)(2,1)S(1)} %collective-permute-done), channel_id=1, source_target_pairs={{64,256},{65,257},{66,258},{67,259},{68,260},{69,261},{70,262},{71... | collective-permute-start | bytes 884744 | tf_op jit(solution)/shard_map/ppermute | solution.py:233
  4.9 1.3 %collective-permute-start.3 = (bf16[224,512]{1,0:T(8,128)(2,1)}, bf16[224,512]{1,0:T(8,128)(2,1)S(1)}, u32[]{:S(2)}, u32[]{:S(2)}) collective-permute-start(bf16[224,512]{1,0:T(8,128)(2,1)} %get-tuple-element.13), channel_id=1, source_target_pairs={{192,256},{193,257},{194,258},{195,259},{196,260},{197,261},{198,2... | collective-permute-start | bytes 688136 | tf_op jit(solution)/shard_map/ppermute | solution.py:233
  6.3 0.7 %slice.3 = s32[512,1]{0,1:T(1,128)S(1)} slice(s32[512,2]{0,1:T(2,128)} %param.7), slice={[0:512], [0:1]} | slice | bytes 4096 | tf_op jit(solution)/shard_map/slice | solution.py:247
  7.0 0.1 stack.35.meta.meta_ref
  7.0 0.0 copy-start
  7.0 0.0 copy-start.1
  7.1 0.0 copy-start.2
  7.1 3.8 %collective-permute-start.6 = (bf16[512,512]{1,0:T(8,128)(2,1)}, bf16[512,512]{1,0:T(8,128)(2,1)S(1)}, u32[]{:S(2)}, u32[]{:S(2)}) collective-permute-start(bf16[512,512]{1,0:T(8,128)(2,1)} %get-tuple-element.12), channel_id=1, source_target_pairs={{0,1},{1,2},{2,3},{3,4},{4,5},{5,6},{6,7},{7,8},{8,9},{9,10},{10,1... | collective-permute-start | bytes 1572872 | tf_op jit(solution)/shard_map/ppermute | solution.py:258
  10.9 2.0 %collective-permute-start.4 = (bf16[512,512]{1,0:T(8,128)(2,1)}, bf16[512,512]{1,0:T(8,128)(2,1)S(1)}, u32[]{:S(2)}, u32[]{:S(2)}) collective-permute-start(bf16[512,512]{1,0:T(8,128)(2,1)} %get-tuple-element.12), channel_id=1, source_target_pairs={{0,64},{1,65},{2,66},{3,67},{4,68},{5,69},{6,70},{7,71},{8,72},{9,... | collective-permute-start | bytes 1572872 | tf_op jit(solution)/shard_map/ppermute | solution.py:233
  12.9 1.3 %collective-permute-start.1 = (bf16[512,512]{1,0:T(8,128)(2,1)}, bf16[512,512]{1,0:T(8,128)(2,1)S(1)}, u32[]{:S(2)}, u32[]{:S(2)}) collective-permute-start(bf16[512,512]{1,0:T(8,128)(2,1)} %get-tuple-element.12), channel_id=1, source_target_pairs={{0,32},{1,33},{2,34},{3,35},{4,36},{5,37},{6,38},{7,39},{8,40},{9,... | collective-permute-start | bytes 1572872 | tf_op jit(solution)/shard_map/ppermute | solution.py:233
  14.2 30.7 %collective-permute-done.3.lower = bf16[224,512]{1,0:T(8,128)(2,1)S(1)} collective-permute-done((bf16[224,512]{1,0:T(8,128)(2,1)}, bf16[224,512]{1,0:T(8,128)(2,1)S(1)}, u32[]{:S(2)}, u32[]{:S(2)}) %collective-permute-start.3) | collective-permute-done | bytes 229408 | tf_op jit(solution)/shard_map/ppermute | solution.py:233
  44.9 5.2 %collective-permute-done.2.upper = bf16[288,512]{1,0:T(8,128)(2,1)S(1)} collective-permute-done((bf16[288,512]{1,0:T(8,128)(2,1)S(1)}, bf16[288,512]{1,0:T(8,128)(2,1)S(1)}, u32[]{:S(2)}, u32[]{:S(2)}) %collective-permute-start.2) | collective-permute-done | bytes 294944 | tf_op jit(solution)/shard_map/ppermute | solution.py:233
  50.1 0.0 collective-permute-done.4.second
  50.1 0.6 choose.1.refs_4_
  50.7 5.9 %collective-permute-start.5 = (bf16[512,512]{1,0:T(8,128)(2,1)S(1)}, bf16[512,512]{1,0:T(8,128)(2,1)S(1)}, u32[]{:S(2)}, u32[]{:S(2)}) collective-permute-start(bf16[512,512]{1,0:T(8,128)(2,1)S(1)} %choose.1.refs_4_), channel_id=1, source_target_pairs={{32,0},{33,1},{34,2},{35,3},{36,4},{37,5},{38,6},{39,7},{40,8},{41... | collective-permute-start | bytes 1572872 | tf_op jit(solution)/shard_map/ppermute | solution.py:233
  56.7 0.0 collective-permute-done.6.refs_5_
  56.7 0.0 collective-permute-done.1.refs_2_
  56.7 1.5 %collective-permute-done.5.refs_3_ = bf16[512,512]{1,0:T(8,128)(2,1)S(1)} collective-permute-done((bf16[512,512]{1,0:T(8,128)(2,1)S(1)}, bf16[512,512]{1,0:T(8,128)(2,1)S(1)}, u32[]{:S(2)}, u32[]{:S(2)}) %collective-permute-start.5) | collective-permute-done | bytes 524320 | tf_op jit(solution)/shard_map/ppermute | solution.py:233
  58.1 0.0 copy-done
  58.2 0.0 copy-done.1
  58.2 0.0 copy-done.2
  58.2 10.4 %attention.1 = (bf16[256,4096]{1,0:T(8,128)(2,1)}, f32[32,256]{1,0:T(8,128)}) custom-call(s32[6]{0:T(128)S(1)} %stack.35.meta.meta_ref, s32[512]{0:T(512)S(1)} %bitcast.7, bf16[256,4096]{1,0:T(8,128)(2,1)S(1)} %copy-done.2, bf16[256,512]{1,0:T(8,128)(2,1)S(1)} %copy-done, bf16[256,512]{1,0:T(8,128)(2,1)S(1)} %copy-done.1, ...), custom_call_target="tpu_custom_call" | custom-call | flops 2400000000 | bytes 8000000 | tf_op jit(solution)/shard_map/attention/pallas_call | solution.py:201
  (1 shorter events, 0.0 us)
Async XLA Ops:
  2.9 0.7 %collective-permute-start = (bf16[288,512]{1,0:T(8,128)(2,1)}, bf16[288,512]{1,0:T(8,128)(2,1)S(1)}, u32[]{:S(2)}, u32[]{:S(2)}) collective-permute-start(bf16[288,512]{1,0:T(8,128)(2,1)} %get-tuple-element.11), channel_id=1, source_target_pairs={{192,64},{193,65},{194,66},{195,67},{196,68},{197,69},{198,70},{19... | collective-permute-start | bytes 884744 | tf_op jit(solution)/shard_map/ppermute | solution.py:233
  3.6 46.5 %collective-permute-start.2 = (bf16[288,512]{1,0:T(8,128)(2,1)S(1)}, bf16[288,512]{1,0:T(8,128)(2,1)S(1)}, u32[]{:S(2)}, u32[]{:S(2)}) collective-permute-start(bf16[288,512]{1,0:T(8,128)(2,1)S(1)} %collective-permute-done), channel_id=1, source_target_pairs={{64,256},{65,257},{66,258},{67,259},{68,260},{69,261},{70,262},{71... | collective-permute-start | bytes 884744 | tf_op jit(solution)/shard_map/ppermute | solution.py:233
  4.9 40.0 %collective-permute-start.3 = (bf16[224,512]{1,0:T(8,128)(2,1)}, bf16[224,512]{1,0:T(8,128)(2,1)S(1)}, u32[]{:S(2)}, u32[]{:S(2)}) collective-permute-start(bf16[224,512]{1,0:T(8,128)(2,1)} %get-tuple-element.13), channel_id=1, source_target_pairs={{192,256},{193,257},{194,258},{195,259},{196,260},{197,261},{198,2... | collective-permute-start | bytes 688136 | tf_op jit(solution)/shard_map/ppermute | solution.py:233
  7.0 51.1 %copy-start = (bf16[256,512]{1,0:T(8,128)(2,1)S(1)}, bf16[256,512]{1,0:T(8,128)(2,1)}, u32[]{:S(2)}) copy-start(bf16[256,512]{1,0:T(8,128)(2,1)} %refs_0_.1) | copy-start | bytes 786436
  7.0 51.1 %copy-start.1 = (bf16[256,512]{1,0:T(8,128)(2,1)S(1)}, bf16[256,512]{1,0:T(8,128)(2,1)}, u32[]{:S(2)}) copy-start(bf16[256,512]{1,0:T(8,128)(2,1)} %refs_1_.1) | copy-start | bytes 786436
  7.1 51.1 %copy-start.2 = (bf16[256,4096]{1,0:T(8,128)(2,1)S(1)}, bf16[256,4096]{1,0:T(8,128)(2,1)}, u32[]{:S(2)}) copy-start(bf16[256,4096]{1,0:T(8,128)(2,1)} %q_ref.1) | copy-start | bytes 6291460
  7.1 49.6 %collective-permute-start.6 = (bf16[512,512]{1,0:T(8,128)(2,1)}, bf16[512,512]{1,0:T(8,128)(2,1)S(1)}, u32[]{:S(2)}, u32[]{:S(2)}) collective-permute-start(bf16[512,512]{1,0:T(8,128)(2,1)} %get-tuple-element.12), channel_id=1, source_target_pairs={{0,1},{1,2},{2,3},{3,4},{4,5},{5,6},{6,7},{7,8},{8,9},{9,10},{10,1... | collective-permute-start | bytes 1572872 | tf_op jit(solution)/shard_map/ppermute | solution.py:258
  10.9 39.2 %collective-permute-start.4 = (bf16[512,512]{1,0:T(8,128)(2,1)}, bf16[512,512]{1,0:T(8,128)(2,1)S(1)}, u32[]{:S(2)}, u32[]{:S(2)}) collective-permute-start(bf16[512,512]{1,0:T(8,128)(2,1)} %get-tuple-element.12), channel_id=1, source_target_pairs={{0,64},{1,65},{2,66},{3,67},{4,68},{5,69},{6,70},{7,71},{8,72},{9,... | collective-permute-start | bytes 1572872 | tf_op jit(solution)/shard_map/ppermute | solution.py:233
  12.9 43.8 %collective-permute-start.1 = (bf16[512,512]{1,0:T(8,128)(2,1)}, bf16[512,512]{1,0:T(8,128)(2,1)S(1)}, u32[]{:S(2)}, u32[]{:S(2)}) collective-permute-start(bf16[512,512]{1,0:T(8,128)(2,1)} %get-tuple-element.12), channel_id=1, source_target_pairs={{0,32},{1,33},{2,34},{3,35},{4,36},{5,37},{6,38},{7,39},{8,40},{9,... | collective-permute-start | bytes 1572872 | tf_op jit(solution)/shard_map/ppermute | solution.py:233
  50.7 7.4 %collective-permute-start.5 = (bf16[512,512]{1,0:T(8,128)(2,1)S(1)}, bf16[512,512]{1,0:T(8,128)(2,1)S(1)}, u32[]{:S(2)}, u32[]{:S(2)}) collective-permute-start(bf16[512,512]{1,0:T(8,128)(2,1)S(1)} %choose.1.refs_4_), channel_id=1, source_target_pairs={{32,0},{33,1},{34,2},{35,3},{36,4},{37,5},{38,6},{39,7},{40,8},{41... | collective-permute-start | bytes 1572872 | tf_op jit(solution)/shard_map/ppermute | solution.py:233

commit v3 on v2

--- a/solution.py
+++ b/solution.py
@@ -139,33 +139,29 @@
     )(*arrays)
 
 
-def pack_body(values, keys, both, relayed, straight, sems):
-    rows, cut = values.shape[0], relayed.shape[0]
+def pack_body(upper, lower, both, sems):
+    rows = upper.shape[0]
     copies = [
-        (values, relayed.at[:rows]),
-        (keys.at[: cut - rows], relayed.at[rows:]),
-        (keys.at[cut - rows :], straight),
-        (values, both.at[:rows]),
-        (keys, both.at[rows:]),
+        pltpu.make_async_copy(upper, both.at[:rows], sems.at[0]),
+        pltpu.make_async_copy(lower, both.at[rows:], sems.at[1]),
     ]
-    copies = [pltpu.make_async_copy(source, to, sems.at[i]) for i, (source, to) in enumerate(copies)]
     for copy in copies:
         copy.start()
     for copy in copies:
         copy.wait()
 
 
-def pack(values, keys, cut):
-    rows, width = keys.shape
+def pack(upper, lower):
+    rows, width = upper.shape
     return pl.pallas_call(
         pack_body,
-        out_shape=[jax.ShapeDtypeStruct((n, width), keys.dtype) for n in (2 * rows, cut, 2 * rows - cut)],
+        out_shape=jax.ShapeDtypeStruct((2 * rows, width), upper.dtype),
         in_specs=[pl.BlockSpec(memory_space=pl.ANY)] * 2,
-        out_specs=[pl.BlockSpec(memory_space=pltpu.VMEM)] * 3,
-        scratch_shapes=[pltpu.SemaphoreType.DMA((5,))],
+        out_specs=pl.BlockSpec(memory_space=pltpu.VMEM),
+        scratch_shapes=[pltpu.SemaphoreType.DMA((2,))],
         compiler_params=pltpu.CompilerParams(vmem_limit_bytes=56 * 2**20),
         name="pack",
-    )(values, keys)
+    )(upper, lower)
 
 
 def join_body(upper, lower, out):
@@ -258,13 +254,12 @@
         return lax.ppermute(block, AXES, route)
 
     rows, width = keys.shape
-    cut = 2 * rows * 9 // 16
-    both, relayed, straight = pack(values, keys, cut)
-    spread = send(relayed, lambda h: [((h, last, 0), (h, 1, 0)), ((h, last, 1), (h, 2, 1))])
-    straight = send(straight, lambda h: [((h, last, c), (h + 1, 0, c)) for c in range(CORES)])
+    spread = send(values, lambda h: [((h, last, 0), (h, 1, 0)), ((h, last, 1), (h, 2, 1))])
+    straight = send(keys, lambda h: [((h, last, c), (h + 1, 0, c)) for c in range(CORES)])
     crossed = send(spread, lambda h: [((h, 1, 0), (h + 1, 0, 0)), ((h, 2, 1), (h + 1, 0, 1))])
     (crossed,) = small_kernel(join_body, "join", JOIN, [(2 * rows, width)], crossed, straight)
-    both, spread = lax.optimization_barrier((both, spread))
+    late_k, late_v, spread = lax.optimization_barrier((keys, values, spread))
+    both = pack(late_v, late_k)
     side = send_outer(both)
     stepped = send(both, lambda h: [((h, y, c), (h, y + 1, c)) for y in range(last) for c in range(CORES)])
     handed = send(both, lambda h: [((h, y, 0), (h, y, 1)) for y in range(Y)])

time: 68.8 us -> 65.8 us (0.956)
  the two profiles are of different devices: /device:TPU:39 before, /device:TPU:25 now
where the time goes in v3:
time: 65.8 us; the launch traced here: 65.6 us
  starting transfers between devices  25.8 us (39%)
  waiting for transfers between devices  25.7 us (39%)
  Pallas kernels  12.4 us (19%)
  between operations  0.85 us (1%)
  local copies, waits for them, and re-layouts  0.79 us (1%)
    ppermute x6, starting transfers between devices, send(): return lax.ppermute(block, AXES, sorted(route))  23 us
    ppermute x6, waiting for transfers between devices, send(): return lax.ppermute(block, AXES, sorted(route))  14.2 us
    ppermute x1, waiting for transfers between devices, send_outer(): return lax.ppermute(block, AXES, route)  11.5 us
    pallas_call x1, Pallas kernels, attention(): pl.pallas_call(body, grid=(width // (GROUP * D),), out_shape=(jax.ShapeDt...  9.98 us
    ppermute x1, starting transfers between devices, send_outer(): return lax.ppermute(block, AXES, route)  2.78 us
    pallas_call x1, Pallas kernels, pack(): pl.pallas_call(pack_body, out_shape=jax.ShapeDtypeStruct((2 * rows, width...  1.84 us
  transfers between devices with their start and end apart: 7, of which 3 were waited for; matrix products, arithmetic and copies ran while one was open for 1% of the time, Pallas kernels for 4%

profile of v3, /device:TPU:25, one launch (start us, length us, event | category | flops | bytes accessed | tf_op | source)
XLA Modules:
  0.0 65.6 jit_solution(7599018245998025092)
XLA Ops:
  0.6 2.4 %collective-permute-start = (bf16[256,512]{1,0:T(8,128)(2,1)}, bf16[256,512]{1,0:T(8,128)(2,1)S(1)}, u32[]{:S(2)}, u32[]{:S(2)}) collective-permute-start(bf16[256,512]{1,0:T(8,128)(2,1)} %refs_1_.1), channel_id=1, source_target_pairs={{192,64},{193,65},{194,66},{195,67},{196,68},{197,69},{198,70},{19... | collective-permute-start | bytes 786440 | tf_op jit(solution)/shard_map/ppermute | solution.py:229
  3.0 13.4 %collective-permute-start.3 = (bf16[256,512]{1,0:T(8,128)(2,1)}, bf16[256,512]{1,0:T(8,128)(2,1)S(1)}, u32[]{:S(2)}, u32[]{:S(2)}) collective-permute-start(bf16[256,512]{1,0:T(8,128)(2,1)} %refs_0_.1), channel_id=1, source_target_pairs={{192,256},{193,257},{194,258},{195,259},{196,260},{197,261},{198,2... | collective-permute-start | bytes 786440 | tf_op jit(solution)/shard_map/ppermute | solution.py:229
  16.4 0.0 collective-permute-done
  16.4 0.7 %collective-permute-start.2 = (bf16[256,512]{1,0:T(8,128)(2,1)S(1)}, bf16[256,512]{1,0:T(8,128)(2,1)S(1)}, u32[]{:S(2)}, u32[]{:S(2)}) collective-permute-start(bf16[256,512]{1,0:T(8,128)(2,1)S(1)} %collective-permute-done), channel_id=1, source_target_pairs={{64,256},{65,257},{66,258},{67,259},{68,260},{69,261},{70,262},{71... | collective-permute-start | bytes 786440 | tf_op jit(solution)/shard_map/ppermute | solution.py:229
  17.2 0.7 %slice.3 = s32[512,1]{0,1:T(1,128)S(1)} slice(s32[512,2]{0,1:T(2,128)} %param.7), slice={[0:512], [0:1]} | slice | bytes 4096 | tf_op jit(solution)/shard_map/slice | solution.py:243
  17.9 0.1 stack.35.meta.meta_ref
  18.0 1.8 %pack.1 = bf16[512,512]{1,0:T(8,128)(2,1)} custom-call(bf16[256,512]{1,0:T(8,128)(2,1)} %refs_1_.1, bf16[256,512]{1,0:T(8,128)(2,1)} %refs_0_.1), custom_call_target="tpu_custom_call" | custom-call | tf_op jit(solution)/shard_map/pack/pallas_call | solution.py:156
  19.8 0.0 copy-start
  19.9 0.0 copy-start.1
  19.9 0.0 copy-start.2
  19.9 2.8 %collective-permute-start.6 = (bf16[512,512]{1,0:T(8,128)(2,1)}, bf16[512,512]{1,0:T(8,128)(2,1)S(1)}, u32[]{:S(2)}, u32[]{:S(2)}) collective-permute-start(bf16[512,512]{1,0:T(8,128)(2,1)} %pack.1), channel_id=1, source_target_pairs={{0,1},{1,2},{2,3},{3,4},{4,5},{5,6},{6,7},{7,8},{8,9},{9,10},{10,1... | collective-permute-start | bytes 1572872 | tf_op jit(solution)/shard_map/ppermute | solution.py:254
  22.7 1.3 %collective-permute-start.4 = (bf16[512,512]{1,0:T(8,128)(2,1)}, bf16[512,512]{1,0:T(8,128)(2,1)S(1)}, u32[]{:S(2)}, u32[]{:S(2)}) collective-permute-start(bf16[512,512]{1,0:T(8,128)(2,1)} %pack.1), channel_id=1, source_target_pairs={{0,64},{1,65},{2,66},{3,67},{4,68},{5,69},{6,70},{7,71},{8,72},{9,... | collective-permute-start | bytes 1572872 | tf_op jit(solution)/shard_map/ppermute | solution.py:229
  24.0 1.3 %collective-permute-start.1 = (bf16[512,512]{1,0:T(8,128)(2,1)}, bf16[512,512]{1,0:T(8,128)(2,1)S(1)}, u32[]{:S(2)}, u32[]{:S(2)}) collective-permute-start(bf16[512,512]{1,0:T(8,128)(2,1)} %pack.1), channel_id=1, source_target_pairs={{0,32},{1,33},{2,34},{3,35},{4,36},{5,37},{6,38},{7,39},{8,40},{9,... | collective-permute-start | bytes 1572872 | tf_op jit(solution)/shard_map/ppermute | solution.py:229
  25.3 4.5 %collective-permute-done.3.lower = bf16[256,512]{1,0:T(8,128)(2,1)S(1)} collective-permute-done((bf16[256,512]{1,0:T(8,128)(2,1)}, bf16[256,512]{1,0:T(8,128)(2,1)S(1)}, u32[]{:S(2)}, u32[]{:S(2)}) %collective-permute-start.3) | collective-permute-done | bytes 262176 | tf_op jit(solution)/shard_map/ppermute | solution.py:229
  29.7 0.0 collective-permute-done.2.upper
  29.8 9.7 %collective-permute-done.4.second = bf16[512,512]{1,0:T(8,128)(2,1)S(1)} collective-permute-done((bf16[512,512]{1,0:T(8,128)(2,1)}, bf16[512,512]{1,0:T(8,128)(2,1)S(1)}, u32[]{:S(2)}, u32[]{:S(2)}) %collective-permute-start.4) | collective-permute-done | bytes 524320 | tf_op jit(solution)/shard_map/ppermute | solution.py:229
  39.5 0.6 choose.1.refs_4_
  40.1 4.0 %collective-permute-start.5 = (bf16[512,512]{1,0:T(8,128)(2,1)S(1)}, bf16[512,512]{1,0:T(8,128)(2,1)S(1)}, u32[]{:S(2)}, u32[]{:S(2)}) collective-permute-start(bf16[512,512]{1,0:T(8,128)(2,1)S(1)} %choose.1.refs_4_), channel_id=1, source_target_pairs={{32,0},{33,1},{34,2},{35,3},{36,4},{37,5},{38,6},{39,7},{40,8},{41... | collective-permute-start | bytes 1572872 | tf_op jit(solution)/shard_map/ppermute | solution.py:229
  44.1 11.5 %collective-permute-done.6.refs_5_ = bf16[512,512]{1,0:T(8,128)(2,1)S(1)} collective-permute-done((bf16[512,512]{1,0:T(8,128)(2,1)}, bf16[512,512]{1,0:T(8,128)(2,1)S(1)}, u32[]{:S(2)}, u32[]{:S(2)}) %collective-permute-start.6) | collective-permute-done | bytes 524320 | tf_op jit(solution)/shard_map/ppermute | solution.py:254
  55.5 0.0 collective-permute-done.1.refs_2_
  55.6 0.0 collective-permute-done.5.refs_3_
  55.6 0.0 copy-done
  55.6 0.0 copy-done.1
  55.6 0.0 copy-done.2
  55.6 10.0 %attention.1 = (bf16[256,4096]{1,0:T(8,128)(2,1)}, f32[32,256]{1,0:T(8,128)}) custom-call(s32[6]{0:T(128)S(1)} %stack.35.meta.meta_ref, s32[512]{0:T(512)S(1)} %bitcast.7, bf16[256,4096]{1,0:T(8,128)(2,1)S(1)} %copy-done.2, bf16[256,512]{1,0:T(8,128)(2,1)S(1)} %copy-done, bf16[256,512]{1,0:T(8,128)(2,1)S(1)} %copy-done.1, ...), custom_call_target="tpu_custom_call" | custom-call | flops 2400000000 | bytes 8000000 | tf_op jit(solution)/shard_map/attention/pallas_call | solution.py:197
  (1 shorter events, 0.0 us)
Async XLA Ops:
  0.6 15.8 %collective-permute-start = (bf16[256,512]{1,0:T(8,128)(2,1)}, bf16[256,512]{1,0:T(8,128)(2,1)S(1)}, u32[]{:S(2)}, u32[]{:S(2)}) collective-permute-start(bf16[256,512]{1,0:T(8,128)(2,1)} %refs_1_.1), channel_id=1, source_target_pairs={{192,64},{193,65},{194,66},{195,67},{196,68},{197,69},{198,70},{19... | collective-permute-start | bytes 786440 | tf_op jit(solution)/shard_map/ppermute | solution.py:229
  3.0 26.7 %collective-permute-start.3 = (bf16[256,512]{1,0:T(8,128)(2,1)}, bf16[256,512]{1,0:T(8,128)(2,1)S(1)}, u32[]{:S(2)}, u32[]{:S(2)}) collective-permute-start(bf16[256,512]{1,0:T(8,128)(2,1)} %refs_0_.1), channel_id=1, source_target_pairs={{192,256},{193,257},{194,258},{195,259},{196,260},{197,261},{198,2... | collective-permute-start | bytes 786440 | tf_op jit(solution)/shard_map/ppermute | solution.py:229
  16.4 13.3 %collective-permute-start.2 = (bf16[256,512]{1,0:T(8,128)(2,1)S(1)}, bf16[256,512]{1,0:T(8,128)(2,1)S(1)}, u32[]{:S(2)}, u32[]{:S(2)}) collective-permute-start(bf16[256,512]{1,0:T(8,128)(2,1)S(1)} %collective-permute-done), channel_id=1, source_target_pairs={{64,256},{65,257},{66,258},{67,259},{68,260},{69,261},{70,262},{71... | collective-permute-start | bytes 786440 | tf_op jit(solution)/shard_map/ppermute | solution.py:229
  19.8 35.7 %copy-start = (bf16[256,512]{1,0:T(8,128)(2,1)S(1)}, bf16[256,512]{1,0:T(8,128)(2,1)}, u32[]{:S(2)}) copy-start(bf16[256,512]{1,0:T(8,128)(2,1)} %refs_0_.1) | copy-start | bytes 786436
  19.9 35.7 %copy-start.1 = (bf16[256,512]{1,0:T(8,128)(2,1)S(1)}, bf16[256,512]{1,0:T(8,128)(2,1)}, u32[]{:S(2)}) copy-start(bf16[256,512]{1,0:T(8,128)(2,1)} %refs_1_.1) | copy-start | bytes 786436
  19.9 35.7 %copy-start.2 = (bf16[256,4096]{1,0:T(8,128)(2,1)S(1)}, bf16[256,4096]{1,0:T(8,128)(2,1)}, u32[]{:S(2)}) copy-start(bf16[256,4096]{1,0:T(8,128)(2,1)} %q_ref.1) | copy-start | bytes 6291460
  19.9 35.7 %collective-permute-start.6 = (bf16[512,512]{1,0:T(8,128)(2,1)}, bf16[512,512]{1,0:T(8,128)(2,1)S(1)}, u32[]{:S(2)}, u32[]{:S(2)}) collective-permute-start(bf16[512,512]{1,0:T(8,128)(2,1)} %pack.1), channel_id=1, source_target_pairs={{0,1},{1,2},{2,3},{3,4},{4,5},{5,6},{6,7},{7,8},{8,9},{9,10},{10,1... | collective-permute-start | bytes 1572872 | tf_op jit(solution)/shard_map/ppermute | solution.py:254
  22.7 16.8 %collective-permute-start.4 = (bf16[512,512]{1,0:T(8,128)(2,1)}, bf16[512,512]{1,0:T(8,128)(2,1)S(1)}, u32[]{:S(2)}, u32[]{:S(2)}) collective-permute-start(bf16[512,512]{1,0:T(8,128)(2,1)} %pack.1), channel_id=1, source_target_pairs={{0,64},{1,65},{2,66},{3,67},{4,68},{5,69},{6,70},{7,71},{8,72},{9,... | collective-permute-start | bytes 1572872 | tf_op jit(solution)/shard_map/ppermute | solution.py:229
  24.0 31.6 %collective-permute-start.1 = (bf16[512,512]{1,0:T(8,128)(2,1)}, bf16[512,512]{1,0:T(8,128)(2,1)S(1)}, u32[]{:S(2)}, u32[]{:S(2)}) collective-permute-start(bf16[512,512]{1,0:T(8,128)(2,1)} %pack.1), channel_id=1, source_target_pairs={{0,32},{1,33},{2,34},{3,35},{4,36},{5,37},{6,38},{7,39},{8,40},{9,... | collective-permute-start | bytes 1572872 | tf_op jit(solution)/shard_map/ppermute | solution.py:229
  40.1 15.5 %collective-permute-start.5 = (bf16[512,512]{1,0:T(8,128)(2,1)S(1)}, bf16[512,512]{1,0:T(8,128)(2,1)S(1)}, u32[]{:S(2)}, u32[]{:S(2)}) collective-permute-start(bf16[512,512]{1,0:T(8,128)(2,1)S(1)} %choose.1.refs_4_), channel_id=1, source_target_pairs={{32,0},{33,1},{34,2},{35,3},{36,4},{37,5},{38,6},{39,7},{40,8},{41... | collective-permute-start | bytes 1572872 | tf_op jit(solution)/shard_map/ppermute | solution.py:229

commit v4 on v3

--- a/solution.py
+++ b/solution.py
@@ -164,10 +164,11 @@
     )(upper, lower)
 
 
-def join_body(upper, lower, out):
-    rows = upper.shape[0]
+def join_body(upper, middle, lower, out):
+    rows, half = upper.shape[0], middle.shape[0]
     out[:rows, :] = upper[...]
-    out[rows:, :] = lower[...]
+    out[rows : rows + half, :] = middle[...]
+    out[rows + half :, :] = lower[...]
 
 
 def choose_body(meta, first, second, out):
@@ -255,9 +256,11 @@
 
     rows, width = keys.shape
     spread = send(values, lambda h: [((h, last, 0), (h, 1, 0)), ((h, last, 1), (h, 2, 1))])
-    straight = send(keys, lambda h: [((h, last, c), (h + 1, 0, c)) for c in range(CORES)])
+    straight = send(keys[: rows // 2], lambda h: [((h, last, c), (h + 1, 0, c)) for c in range(CORES)])
+    spread_k = send(keys[rows // 2 :], lambda h: [((h, last, c), (h, 0, c)) for c in range(CORES)])
+    turned = send(spread_k, lambda h: [((h, 0, c), (h + 1, 0, c)) for c in range(CORES)])
     crossed = send(spread, lambda h: [((h, 1, 0), (h + 1, 0, 0)), ((h, 2, 1), (h + 1, 0, 1))])
-    (crossed,) = small_kernel(join_body, "join", JOIN, [(2 * rows, width)], crossed, straight)
+    (crossed,) = small_kernel(join_body, "join", JOIN, [(2 * rows, width)], crossed, straight, turned)
     late_k, late_v, spread = lax.optimization_barrier((keys, values, spread))
     both = pack(late_v, late_k)
     side = send_outer(both)

time: 65.8 us -> 64 us (0.973)
  the two profiles are of different devices: /device:TPU:25 before, /device:TPU:39 now
where the time goes in v4:
time: 64 us; the launch traced here: 63.5 us
  starting transfers between devices  35.2 us (55%)
  waiting for transfers between devices  13.2 us (21%)
  Pallas kernels  12.4 us (19%)
  local copies, waits for them, and re-layouts  1.78 us (3%)
  between operations  0.87 us (1%)
    ppermute x8, starting transfers between devices, send(): return lax.ppermute(block, AXES, sorted(route))  32.5 us
    ppermute x8, waiting for transfers between devices, send(): return lax.ppermute(block, AXES, sorted(route))  13.2 us
    pallas_call x1, Pallas kernels, attention(): pl.pallas_call(body, grid=(width // (GROUP * D),), out_shape=(jax.ShapeDt...  9.97 us
    ppermute x1, starting transfers between devices, send_outer(): return lax.ppermute(block, AXES, route)  2.78 us
    pallas_call x1, Pallas kernels, pack(): pl.pallas_call(pack_body, out_shape=jax.ShapeDtypeStruct((2 * rows, width...  1.84 us
  transfers between devices with their start and end apart: 9, of which 5 were waited for; matrix products, arithmetic and copies ran while one was open for 3% of the time, Pallas kernels for 4%

profile of v4, /device:TPU:39, one launch (start us, length us, event | category | flops | bytes accessed | tf_op | source)
XLA Modules:
  0.0 63.5 jit_solution(1430967120393794555)
XLA Ops:
  0.6 0.7 %collective-permute-start = (bf16[256,512]{1,0:T(8,128)(2,1)}, bf16[256,512]{1,0:T(8,128)(2,1)S(1)}, u32[]{:S(2)}, u32[]{:S(2)}) collective-permute-start(bf16[256,512]{1,0:T(8,128)(2,1)} %refs_1_.1), channel_id=1, source_target_pairs={{192,64},{193,65},{194,66},{195,67},{196,68},{197,69},{198,70},{19... | collective-permute-start | bytes 786440 | tf_op jit(solution)/shard_map/ppermute | solution.py:230
  1.3 1.0 %fusion = (bf16[128,512]{1,0:T(8,128)(2,1)S(1)}, bf16[128,512]{1,0:T(8,128)(2,1)S(1)}) fusion(bf16[256,512]{1,0:T(8,128)(2,1)} %refs_0_.1), kind=kLoop, calls=%fused_computation | loop fusion | bytes 524288 | tf_op jit(solution)/shard_map/slice | solution.py:260
  2.3 1.3 %collective-permute-start.4 = (bf16[128,512]{1,0:T(8,128)(2,1)S(1)}, bf16[128,512]{1,0:T(8,128)(2,1)S(1)}, u32[]{:S(2)}, u32[]{:S(2)}) collective-permute-start(bf16[128,512]{1,0:T(8,128)(2,1)S(1)} %get-tuple-element.10), channel_id=1, source_target_pairs={{192,0},{193,1},{194,2},{195,3},{196,4},{197,5},{198,6},{199,7},{2... | collective-permute-start | bytes 393224 | tf_op jit(solution)/shard_map/ppermute | solution.py:230
  3.6 0.0 collective-permute-done
  3.6 1.3 %collective-permute-start.2 = (bf16[256,512]{1,0:T(8,128)(2,1)S(1)}, bf16[256,512]{1,0:T(8,128)(2,1)S(1)}, u32[]{:S(2)}, u32[]{:S(2)}) collective-permute-start(bf16[256,512]{1,0:T(8,128)(2,1)S(1)} %collective-permute-done), channel_id=1, source_target_pairs={{64,256},{65,257},{66,258},{67,259},{68,260},{69,261},{70,262},{71... | collective-permute-start | bytes 786440 | tf_op jit(solution)/shard_map/ppermute | solution.py:230
  4.9 1.3 %collective-permute-start.3 = (bf16[128,512]{1,0:T(8,128)(2,1)S(1)}, bf16[128,512]{1,0:T(8,128)(2,1)S(1)}, u32[]{:S(2)}, u32[]{:S(2)}) collective-permute-start(bf16[128,512]{1,0:T(8,128)(2,1)S(1)} %get-tuple-element.11), channel_id=1, source_target_pairs={{192,256},{193,257},{194,258},{195,259},{196,260},{197,261},{198,2... | collective-permute-start | bytes 393224 | tf_op jit(solution)/shard_map/ppermute | solution.py:230
  6.2 4.2 %collective-permute-done.4 = bf16[128,512]{1,0:T(8,128)(2,1)S(1)} collective-permute-done((bf16[128,512]{1,0:T(8,128)(2,1)S(1)}, bf16[128,512]{1,0:T(8,128)(2,1)S(1)}, u32[]{:S(2)}, u32[]{:S(2)}) %collective-permute-start.4) | collective-permute-done | bytes 131104 | tf_op jit(solution)/shard_map/ppermute | solution.py:230
  10.4 14.5 %collective-permute-start.5 = (bf16[128,512]{1,0:T(8,128)(2,1)S(1)}, bf16[128,512]{1,0:T(8,128)(2,1)S(1)}, u32[]{:S(2)}, u32[]{:S(2)}) collective-permute-start(bf16[128,512]{1,0:T(8,128)(2,1)S(1)} %collective-permute-done.4), channel_id=1, source_target_pairs={{0,256},{1,257},{2,258},{3,259},{4,260},{5,261},{6,262},{7,263},{8... | collective-permute-start | bytes 393224 | tf_op jit(solution)/shard_map/ppermute | solution.py:230
  25.0 0.7 %slice.9 = s32[512,1]{0,1:T(1,128)S(1)} slice(s32[512,2]{0,1:T(2,128)} %param.7), slice={[0:512], [0:1]} | slice | bytes 4096 | tf_op jit(solution)/shard_map/slice | solution.py:244
  25.7 0.1 stack.35.meta.meta_ref
  25.8 1.8 %pack.1 = bf16[512,512]{1,0:T(8,128)(2,1)} custom-call(bf16[256,512]{1,0:T(8,128)(2,1)} %refs_1_.1, bf16[256,512]{1,0:T(8,128)(2,1)} %refs_0_.1), custom_call_target="tpu_custom_call" | custom-call | tf_op jit(solution)/shard_map/pack/pallas_call | solution.py:156
  27.6 0.0 copy-start
  27.6 0.0 copy-start.1
  27.7 0.0 copy-start.2
  27.7 2.8 %collective-permute-start.8 = (bf16[512,512]{1,0:T(8,128)(2,1)}, bf16[512,512]{1,0:T(8,128)(2,1)S(1)}, u32[]{:S(2)}, u32[]{:S(2)}) collective-permute-start(bf16[512,512]{1,0:T(8,128)(2,1)} %pack.1), channel_id=1, source_target_pairs={{0,1},{1,2},{2,3},{3,4},{4,5},{5,6},{6,7},{7,8},{8,9},{9,10},{10,1... | collective-permute-start | bytes 1572872 | tf_op jit(solution)/shard_map/ppermute | solution.py:255
  30.5 1.3 %collective-permute-start.6 = (bf16[512,512]{1,0:T(8,128)(2,1)}, bf16[512,512]{1,0:T(8,128)(2,1)S(1)}, u32[]{:S(2)}, u32[]{:S(2)}) collective-permute-start(bf16[512,512]{1,0:T(8,128)(2,1)} %pack.1), channel_id=1, source_target_pairs={{0,64},{1,65},{2,66},{3,67},{4,68},{5,69},{6,70},{7,71},{8,72},{9,... | collective-permute-start | bytes 1572872 | tf_op jit(solution)/shard_map/ppermute | solution.py:230
  31.8 2.4 %collective-permute-done.3.middle = bf16[128,512]{1,0:T(8,128)(2,1)S(1)} collective-permute-done((bf16[128,512]{1,0:T(8,128)(2,1)S(1)}, bf16[128,512]{1,0:T(8,128)(2,1)S(1)}, u32[]{:S(2)}, u32[]{:S(2)}) %collective-permute-start.3) | collective-permute-done | bytes 131104 | tf_op jit(solution)/shard_map/ppermute | solution.py:230
  34.1 1.3 %collective-permute-start.1 = (bf16[512,512]{1,0:T(8,128)(2,1)}, bf16[512,512]{1,0:T(8,128)(2,1)S(1)}, u32[]{:S(2)}, u32[]{:S(2)}) collective-permute-start(bf16[512,512]{1,0:T(8,128)(2,1)} %pack.1), channel_id=1, source_target_pairs={{0,32},{1,33},{2,34},{3,35},{4,36},{5,37},{6,38},{7,39},{8,40},{9,... | collective-permute-start | bytes 1572872 | tf_op jit(solution)/shard_map/ppermute | solution.py:230
  35.4 0.0 collective-permute-done.5.lower
  35.4 2.7 %collective-permute-done.2.upper = bf16[256,512]{1,0:T(8,128)(2,1)S(1)} collective-permute-done((bf16[256,512]{1,0:T(8,128)(2,1)S(1)}, bf16[256,512]{1,0:T(8,128)(2,1)S(1)}, u32[]{:S(2)}, u32[]{:S(2)}) %collective-permute-start.2) | collective-permute-done | bytes 262176 | tf_op jit(solution)/shard_map/ppermute | solution.py:230
  38.2 2.5 %collective-permute-done.6.second = bf16[512,512]{1,0:T(8,128)(2,1)S(1)} collective-permute-done((bf16[512,512]{1,0:T(8,128)(2,1)}, bf16[512,512]{1,0:T(8,128)(2,1)S(1)}, u32[]{:S(2)}, u32[]{:S(2)}) %collective-permute-start.6) | collective-permute-done | bytes 524320 | tf_op jit(solution)/shard_map/ppermute | solution.py:230
  40.7 0.6 choose.1.refs_4_
  41.3 10.8 %collective-permute-start.7 = (bf16[512,512]{1,0:T(8,128)(2,1)S(1)}, bf16[512,512]{1,0:T(8,128)(2,1)S(1)}, u32[]{:S(2)}, u32[]{:S(2)}) collective-permute-start(bf16[512,512]{1,0:T(8,128)(2,1)S(1)} %choose.1.refs_4_), channel_id=1, source_target_pairs={{32,0},{33,1},{34,2},{35,3},{36,4},{37,5},{38,6},{39,7},{40,8},{41... | collective-permute-start | bytes 1572872 | tf_op jit(solution)/shard_map/ppermute | solution.py:230
  52.0 0.0 collective-permute-done.8.refs_5_
  52.0 0.0 collective-permute-done.1.refs_2_
  52.1 1.5 %collective-permute-done.7.refs_3_ = bf16[512,512]{1,0:T(8,128)(2,1)S(1)} collective-permute-done((bf16[512,512]{1,0:T(8,128)(2,1)S(1)}, bf16[512,512]{1,0:T(8,128)(2,1)S(1)}, u32[]{:S(2)}, u32[]{:S(2)}) %collective-permute-start.7) | collective-permute-done | bytes 524320 | tf_op jit(solution)/shard_map/ppermute | solution.py:230
  53.5 0.0 copy-done
  53.5 0.0 copy-done.1
  53.5 0.0 copy-done.2
  53.5 10.0 %attention.1 = (bf16[256,4096]{1,0:T(8,128)(2,1)}, f32[32,256]{1,0:T(8,128)}) custom-call(s32[6]{0:T(128)S(1)} %stack.35.meta.meta_ref, s32[512]{0:T(512)S(1)} %bitcast.7, bf16[256,4096]{1,0:T(8,128)(2,1)S(1)} %copy-done.2, bf16[256,512]{1,0:T(8,128)(2,1)S(1)} %copy-done, bf16[256,512]{1,0:T(8,128)(2,1)S(1)} %copy-done.1, ...), custom_call_target="tpu_custom_call" | custom-call | flops 2400000000 | bytes 8000000 | tf_op jit(solution)/shard_map/attention/pallas_call | solution.py:198
  (1 shorter events, 0.0 us)
Async XLA Ops:
  0.6 3.0 %collective-permute-start = (bf16[256,512]{1,0:T(8,128)(2,1)}, bf16[256,512]{1,0:T(8,128)(2,1)S(1)}, u32[]{:S(2)}, u32[]{:S(2)}) collective-permute-start(bf16[256,512]{1,0:T(8,128)(2,1)} %refs_1_.1), channel_id=1, source_target_pairs={{192,64},{193,65},{194,66},{195,67},{196,68},{197,69},{198,70},{19... | collective-permute-start | bytes 786440 | tf_op jit(solution)/shard_map/ppermute | solution.py:230
  2.3 8.1 %collective-permute-start.4 = (bf16[128,512]{1,0:T(8,128)(2,1)S(1)}, bf16[128,512]{1,0:T(8,128)(2,1)S(1)}, u32[]{:S(2)}, u32[]{:S(2)}) collective-permute-start(bf16[128,512]{1,0:T(8,128)(2,1)S(1)} %get-tuple-element.10), channel_id=1, source_target_pairs={{192,0},{193,1},{194,2},{195,3},{196,4},{197,5},{198,6},{199,7},{2... | collective-permute-start | bytes 393224 | tf_op jit(solution)/shard_map/ppermute | solution.py:230
  3.6 34.5 %collective-permute-start.2 = (bf16[256,512]{1,0:T(8,128)(2,1)S(1)}, bf16[256,512]{1,0:T(8,128)(2,1)S(1)}, u32[]{:S(2)}, u32[]{:S(2)}) collective-permute-start(bf16[256,512]{1,0:T(8,128)(2,1)S(1)} %collective-permute-done), channel_id=1, source_target_pairs={{64,256},{65,257},{66,258},{67,259},{68,260},{69,261},{70,262},{71... | collective-permute-start | bytes 786440 | tf_op jit(solution)/shard_map/ppermute | solution.py:230
  4.9 29.2 %collective-permute-start.3 = (bf16[128,512]{1,0:T(8,128)(2,1)S(1)}, bf16[128,512]{1,0:T(8,128)(2,1)S(1)}, u32[]{:S(2)}, u32[]{:S(2)}) collective-permute-start(bf16[128,512]{1,0:T(8,128)(2,1)S(1)} %get-tuple-element.11), channel_id=1, source_target_pairs={{192,256},{193,257},{194,258},{195,259},{196,260},{197,261},{198,2... | collective-permute-start | bytes 393224 | tf_op jit(solution)/shard_map/ppermute | solution.py:230
  10.4 25.1 %collective-permute-start.5 = (bf16[128,512]{1,0:T(8,128)(2,1)S(1)}, bf16[128,512]{1,0:T(8,128)(2,1)S(1)}, u32[]{:S(2)}, u32[]{:S(2)}) collective-permute-start(bf16[128,512]{1,0:T(8,128)(2,1)S(1)} %collective-permute-done.4), channel_id=1, source_target_pairs={{0,256},{1,257},{2,258},{3,259},{4,260},{5,261},{6,262},{7,263},{8... | collective-permute-start | bytes 393224 | tf_op jit(solution)/shard_map/ppermute | solution.py:230
  27.6 25.9 %copy-start = (bf16[256,512]{1,0:T(8,128)(2,1)S(1)}, bf16[256,512]{1,0:T(8,128)(2,1)}, u32[]{:S(2)}) copy-start(bf16[256,512]{1,0:T(8,128)(2,1)} %refs_0_.1) | copy-start | bytes 786436
  27.6 25.9 %copy-start.1 = (bf16[256,512]{1,0:T(8,128)(2,1)S(1)}, bf16[256,512]{1,0:T(8,128)(2,1)}, u32[]{:S(2)}) copy-start(bf16[256,512]{1,0:T(8,128)(2,1)} %refs_1_.1) | copy-start | bytes 786436
  27.7 25.9 %copy-start.2 = (bf16[256,4096]{1,0:T(8,128)(2,1)S(1)}, bf16[256,4096]{1,0:T(8,128)(2,1)}, u32[]{:S(2)}) copy-start(bf16[256,4096]{1,0:T(8,128)(2,1)} %q_ref.1) | copy-start | bytes 6291460
  27.7 24.4 %collective-permute-start.8 = (bf16[512,512]{1,0:T(8,128)(2,1)}, bf16[512,512]{1,0:T(8,128)(2,1)S(1)}, u32[]{:S(2)}, u32[]{:S(2)}) collective-permute-start(bf16[512,512]{1,0:T(8,128)(2,1)} %pack.1), channel_id=1, source_target_pairs={{0,1},{1,2},{2,3},{3,4},{4,5},{5,6},{6,7},{7,8},{8,9},{9,10},{10,1... | collective-permute-start | bytes 1572872 | tf_op jit(solution)/shard_map/ppermute | solution.py:255
  30.5 10.2 %collective-permute-start.6 = (bf16[512,512]{1,0:T(8,128)(2,1)}, bf16[512,512]{1,0:T(8,128)(2,1)S(1)}, u32[]{:S(2)}, u32[]{:S(2)}) collective-permute-start(bf16[512,512]{1,0:T(8,128)(2,1)} %pack.1), channel_id=1, source_target_pairs={{0,64},{1,65},{2,66},{3,67},{4,68},{5,69},{6,70},{7,71},{8,72},{9,... | collective-permute-start | bytes 1572872 | tf_op jit(solution)/shard_map/ppermute | solution.py:230
  34.1 17.9 %collective-permute-start.1 = (bf16[512,512]{1,0:T(8,128)(2,1)}, bf16[512,512]{1,0:T(8,128)(2,1)S(1)}, u32[]{:S(2)}, u32[]{:S(2)}) collective-permute-start(bf16[512,512]{1,0:T(8,128)(2,1)} %pack.1), channel_id=1, source_target_pairs={{0,32},{1,33},{2,34},{3,35},{4,36},{5,37},{6,38},{7,39},{8,40},{9,... | collective-permute-start | bytes 1572872 | tf_op jit(solution)/shard_map/ppermute | solution.py:230
  41.3 12.3 %collective-permute-start.7 = (bf16[512,512]{1,0:T(8,128)(2,1)S(1)}, bf16[512,512]{1,0:T(8,128)(2,1)S(1)}, u32[]{:S(2)}, u32[]{:S(2)}) collective-permute-start(bf16[512,512]{1,0:T(8,128)(2,1)S(1)} %choose.1.refs_4_), channel_id=1, source_target_pairs={{32,0},{33,1},{34,2},{35,3},{36,4},{37,5},{38,6},{39,7},{40,8},{41... | collective-permute-start | bytes 1572872 | tf_op jit(solution)/shard_map/ppermute | solution.py:230

commit v5 on v4

--- a/solution.py
+++ b/solution.py
@@ -165,10 +165,14 @@
 
 
 def join_body(upper, middle, lower, out):
-    rows, half = upper.shape[0], middle.shape[0]
-    out[:rows, :] = upper[...]
-    out[rows : rows + half, :] = middle[...]
-    out[rows + half :, :] = lower[...]
+    rows, cut = out.shape[0] // 2, upper.shape[0]
+    half = rows // 2
+    more = middle.shape[0] - half
+    out[:cut, :] = upper[...]
+    out[cut : cut + more, :] = middle[half:, :]
+    out[cut + more : rows, :] = lower[half:, :]
+    out[rows : rows + half, :] = middle[:half, :]
+    out[rows + half :, :] = lower[:half, :]
 
 
 def choose_body(meta, first, second, out):
@@ -255,9 +259,13 @@
         return lax.ppermute(block, AXES, route)
 
     rows, width = keys.shape
-    spread = send(values, lambda h: [((h, last, 0), (h, 1, 0)), ((h, last, 1), (h, 2, 1))])
-    straight = send(keys[: rows // 2], lambda h: [((h, last, c), (h + 1, 0, c)) for c in range(CORES)])
-    spread_k = send(keys[rows // 2 :], lambda h: [((h, last, c), (h, 0, c)) for c in range(CORES)])
+    half, cut = rows // 2, rows * 3 // 4
+    middle = (cut + rows) // 2
+    spread = send(values[:cut], lambda h: [((h, last, 0), (h, 1, 0)), ((h, last, 1), (h, 2, 1))])
+    straight = jnp.concatenate([keys[:half], values[cut:middle]], axis=0)
+    straight = send(straight, lambda h: [((h, last, c), (h + 1, 0, c)) for c in range(CORES)])
+    spread_k = jnp.concatenate([keys[half:], values[middle:]], axis=0)
+    spread_k = send(spread_k, lambda h: [((h, last, c), (h, 0, c)) for c in range(CORES)])
     turned = send(spread_k, lambda h: [((h, 0, c), (h + 1, 0, c)) for c in range(CORES)])
     crossed = send(spread, lambda h: [((h, 1, 0), (h + 1, 0, 0)), ((h, 2, 1), (h + 1, 0, 1))])
     (crossed,) = small_kernel(join_body, "join", JOIN, [(2 * rows, width)], crossed, straight, turned)

time: 64 us -> 67.7 us (1.058)
  the two profiles are of different devices: /device:TPU:39 before, /device:TPU:1 now
where the time goes in v5:
time: 67.7 us; the launch traced here: 67.3 us
  starting transfers between devices  31 us (46%)
  waiting for transfers between devices  19.1 us (28%)
  Pallas kernels  12.8 us (19%)
  local copies, waits for them, and re-layouts  3.51 us (5%)
  between operations  0.91 us (1%)
    ppermute x8, starting transfers between devices, send(): return lax.ppermute(block, AXES, sorted(route))  28.2 us
    ppermute x8, waiting for transfers between devices, send(): return lax.ppermute(block, AXES, sorted(route))  13.1 us
    pallas_call x1, Pallas kernels, attention(): pl.pallas_call(body, grid=(width // (GROUP * D),), out_shape=(jax.ShapeDt...  10.4 us
    ppermute x1, waiting for transfers between devices, send_outer(): return lax.ppermute(block, AXES, route)  5.98 us
    ppermute x1, starting transfers between devices, send_outer(): return lax.ppermute(block, AXES, route)  2.78 us
    pallas_call x1, Pallas kernels, pack(): pl.pallas_call(pack_body, out_shape=jax.ShapeDtypeStruct((2 * rows, width...  1.84 us
    slice x2, local copies, waits for them, and re-layouts, local(): spread_k = jnp.concatenate([keys[half:], values[middle:]], axis=0)  1.77 us
  transfers between devices with their start and end apart: 9, of which 3 were waited for; matrix products, arithmetic and copies ran while one was open for 4% of the time, Pallas kernels for 4%

profile of v5, /device:TPU:1, one launch (start us, length us, event | category | flops | bytes accessed | tf_op | source)
XLA Modules:
  0.0 67.3 jit_solution(5685171316693386139)
XLA Ops:
  0.6 0.9 %slice.19 = bf16[192,512]{1,0:T(8,128)(2,1)S(1)} slice(bf16[256,512]{1,0:T(8,128)(2,1)} %refs_1_.1), slice={[0:192], [0:512]} | slice | bytes 393216 | tf_op jit(solution)/shard_map/slice | solution.py:264
  1.6 0.7 %collective-permute-start = (bf16[192,512]{1,0:T(8,128)(2,1)S(1)}, bf16[192,512]{1,0:T(8,128)(2,1)S(1)}, u32[]{:S(2)}, u32[]{:S(2)}) collective-permute-start(bf16[192,512]{1,0:T(8,128)(2,1)S(1)} %slice.19), channel_id=1, source_target_pairs={{192,64},{193,65},{194,66},{195,67},{196,68},{197,69},{198,70},{19... | collective-permute-start | bytes 589832 | tf_op jit(solution)/shard_map/ppermute | solution.py:234
  2.3 1.0 %fusion = (bf16[128,512]{1,0:T(8,128)(2,1)S(1)}, bf16[128,512]{1,0:T(8,128)(2,1)S(1)}) fusion(bf16[256,512]{1,0:T(8,128)(2,1)} %refs_0_.1), kind=kLoop, calls=%fused_computation.2 | loop fusion | bytes 524288 | tf_op jit(solution)/shard_map/slice | solution.py:267
  3.2 0.8 %fusion.1 = (bf16[32,512]{1,0:T(8,128)(2,1)S(1)}, bf16[32,512]{1,0:T(8,128)(2,1)S(1)}) fusion(bf16[256,512]{1,0:T(8,128)(2,1)} %refs_1_.1), kind=kLoop, calls=%fused_computation.3 | loop fusion | bytes 131072 | tf_op jit(solution)/shard_map/slice | solution.py:267
  4.0 1.3 %collective-permute-start.4 = (bf16[160,512]{1,0:T(8,128)(2,1)S(1)}, bf16[160,512]{1,0:T(8,128)(2,1)S(1)}, u32[]{:S(2)}, u32[]{:S(2)}) collective-permute-start(bf16[160,512]{1,0:T(8,128)(2,1)S(1)} %pad_maximum_fusion.1), channel_id=1, source_target_pairs={{192,0},{193,1},{194,2},{195,3},{196,4},{197,5},{198,6},{199,7},{2... | collective-permute-start | bytes 491528 | tf_op jit(solution)/shard_map/ppermute | solution.py:234
  5.3 0.0 collective-permute-done
  5.4 1.3 %collective-permute-start.2 = (bf16[192,512]{1,0:T(8,128)(2,1)S(1)}, bf16[192,512]{1,0:T(8,128)(2,1)S(1)}, u32[]{:S(2)}, u32[]{:S(2)}) collective-permute-start(bf16[192,512]{1,0:T(8,128)(2,1)S(1)} %collective-permute-done), channel_id=1, source_target_pairs={{64,256},{65,257},{66,258},{67,259},{68,260},{69,261},{70,262},{71... | collective-permute-start | bytes 589832 | tf_op jit(solution)/shard_map/ppermute | solution.py:234
  6.7 1.3 %collective-permute-start.3 = (bf16[160,512]{1,0:T(8,128)(2,1)S(1)}, bf16[160,512]{1,0:T(8,128)(2,1)S(1)}, u32[]{:S(2)}, u32[]{:S(2)}) collective-permute-start(bf16[160,512]{1,0:T(8,128)(2,1)S(1)} %pad_maximum_fusion), channel_id=1, source_target_pairs={{192,256},{193,257},{194,258},{195,259},{196,260},{197,261},{198,2... | collective-permute-start | bytes 491528 | tf_op jit(solution)/shard_map/ppermute | solution.py:234
  8.0 5.3 %collective-permute-done.4 = bf16[160,512]{1,0:T(8,128)(2,1)S(1)} collective-permute-done((bf16[160,512]{1,0:T(8,128)(2,1)S(1)}, bf16[160,512]{1,0:T(8,128)(2,1)S(1)}, u32[]{:S(2)}, u32[]{:S(2)}) %collective-permute-start.4) | collective-permute-done | bytes 163872 | tf_op jit(solution)/shard_map/ppermute | solution.py:234
  13.3 15.8 %collective-permute-start.5 = (bf16[160,512]{1,0:T(8,128)(2,1)S(1)}, bf16[160,512]{1,0:T(8,128)(2,1)S(1)}, u32[]{:S(2)}, u32[]{:S(2)}) collective-permute-start(bf16[160,512]{1,0:T(8,128)(2,1)S(1)} %collective-permute-done.4), channel_id=1, source_target_pairs={{0,256},{1,257},{2,258},{3,259},{4,260},{5,261},{6,262},{7,263},{8... | collective-permute-start | bytes 491528 | tf_op jit(solution)/shard_map/ppermute | solution.py:234
  29.2 0.7 %slice.18 = s32[512,1]{0,1:T(1,128)S(1)} slice(s32[512,2]{0,1:T(2,128)} %param.7), slice={[0:512], [0:1]} | slice | bytes 4096 | tf_op jit(solution)/shard_map/slice | solution.py:248
  29.9 0.1 stack.35.meta.meta_ref
  30.0 1.8 %pack.1 = bf16[512,512]{1,0:T(8,128)(2,1)} custom-call(bf16[256,512]{1,0:T(8,128)(2,1)} %refs_1_.1, bf16[256,512]{1,0:T(8,128)(2,1)} %refs_0_.1), custom_call_target="tpu_custom_call" | custom-call | tf_op jit(solution)/shard_map/pack/pallas_call | solution.py:156
  31.8 0.0 copy-start
  31.8 0.0 copy-start.1
  31.8 0.0 copy-start.2
  31.8 2.8 %collective-permute-start.8 = (bf16[512,512]{1,0:T(8,128)(2,1)}, bf16[512,512]{1,0:T(8,128)(2,1)S(1)}, u32[]{:S(2)}, u32[]{:S(2)}) collective-permute-start(bf16[512,512]{1,0:T(8,128)(2,1)} %pack.1), channel_id=1, source_target_pairs={{0,1},{1,2},{2,3},{3,4},{4,5},{5,6},{6,7},{7,8},{8,9},{9,10},{10,1... | collective-permute-start | bytes 1572872 | tf_op jit(solution)/shard_map/ppermute | solution.py:259
  34.6 1.3 %collective-permute-start.6 = (bf16[512,512]{1,0:T(8,128)(2,1)}, bf16[512,512]{1,0:T(8,128)(2,1)S(1)}, u32[]{:S(2)}, u32[]{:S(2)}) collective-permute-start(bf16[512,512]{1,0:T(8,128)(2,1)} %pack.1), channel_id=1, source_target_pairs={{0,64},{1,65},{2,66},{3,67},{4,68},{5,69},{6,70},{7,71},{8,72},{9,... | collective-permute-start | bytes 1572872 | tf_op jit(solution)/shard_map/ppermute | solution.py:234
  36.0 0.0 collective-permute-done.3.middle
  36.0 1.3 %collective-permute-start.1 = (bf16[512,512]{1,0:T(8,128)(2,1)}, bf16[512,512]{1,0:T(8,128)(2,1)S(1)}, u32[]{:S(2)}, u32[]{:S(2)}) collective-permute-start(bf16[512,512]{1,0:T(8,128)(2,1)} %pack.1), channel_id=1, source_target_pairs={{0,32},{1,33},{2,34},{3,35},{4,36},{5,37},{6,38},{7,39},{8,40},{9,... | collective-permute-start | bytes 1572872 | tf_op jit(solution)/shard_map/ppermute | solution.py:234
  37.3 0.0 collective-permute-done.5.lower
  37.3 0.0 collective-permute-done.2.upper
  37.3 7.7 %collective-permute-done.6.second = bf16[512,512]{1,0:T(8,128)(2,1)S(1)} collective-permute-done((bf16[512,512]{1,0:T(8,128)(2,1)}, bf16[512,512]{1,0:T(8,128)(2,1)S(1)}, u32[]{:S(2)}, u32[]{:S(2)}) %collective-permute-start.6) | collective-permute-done | bytes 524320 | tf_op jit(solution)/shard_map/ppermute | solution.py:234
  45.1 0.6 choose.1.refs_4_
  45.7 5.2 %collective-permute-start.7 = (bf16[512,512]{1,0:T(8,128)(2,1)S(1)}, bf16[512,512]{1,0:T(8,128)(2,1)S(1)}, u32[]{:S(2)}, u32[]{:S(2)}) collective-permute-start(bf16[512,512]{1,0:T(8,128)(2,1)S(1)} %choose.1.refs_4_), channel_id=1, source_target_pairs={{32,0},{33,1},{34,2},{35,3},{36,4},{37,5},{38,6},{39,7},{40,8},{41... | collective-permute-start | bytes 1572872 | tf_op jit(solution)/shard_map/ppermute | solution.py:234
  50.9 6.0 %collective-permute-done.8.refs_5_ = bf16[512,512]{1,0:T(8,128)(2,1)S(1)} collective-permute-done((bf16[512,512]{1,0:T(8,128)(2,1)}, bf16[512,512]{1,0:T(8,128)(2,1)S(1)}, u32[]{:S(2)}, u32[]{:S(2)}) %collective-permute-start.8) | collective-permute-done | bytes 524320 | tf_op jit(solution)/shard_map/ppermute | solution.py:259
  56.9 0.0 collective-permute-done.1.refs_2_
  56.9 0.0 collective-permute-done.7.refs_3_
  56.9 0.0 copy-done
  56.9 0.0 copy-done.1
  56.9 0.0 copy-done.2
  56.9 10.4 %attention.1 = (bf16[256,4096]{1,0:T(8,128)(2,1)}, f32[32,256]{1,0:T(8,128)}) custom-call(s32[6]{0:T(128)S(1)} %stack.35.meta.meta_ref, s32[512]{0:T(512)S(1)} %bitcast.7, bf16[256,4096]{1,0:T(8,128)(2,1)S(1)} %copy-done.2, bf16[256,512]{1,0:T(8,128)(2,1)S(1)} %copy-done, bf16[256,512]{1,0:T(8,128)(2,1)S(1)} %copy-done.1, ...), custom_call_target="tpu_custom_call" | custom-call | flops 2400000000 | bytes 8000000 | tf_op jit(solution)/shard_map/attention/pallas_call | solution.py:202
  (3 shorter events, 0.1 us)
Async XLA Ops:
  1.6 3.8 %collective-permute-start = (bf16[192,512]{1,0:T(8,128)(2,1)S(1)}, bf16[192,512]{1,0:T(8,128)(2,1)S(1)}, u32[]{:S(2)}, u32[]{:S(2)}) collective-permute-start(bf16[192,512]{1,0:T(8,128)(2,1)S(1)} %slice.19), channel_id=1, source_target_pairs={{192,64},{193,65},{194,66},{195,67},{196,68},{197,69},{198,70},{19... | collective-permute-start | bytes 589832 | tf_op jit(solution)/shard_map/ppermute | solution.py:234
  4.0 9.3 %collective-permute-start.4 = (bf16[160,512]{1,0:T(8,128)(2,1)S(1)}, bf16[160,512]{1,0:T(8,128)(2,1)S(1)}, u32[]{:S(2)}, u32[]{:S(2)}) collective-permute-start(bf16[160,512]{1,0:T(8,128)(2,1)S(1)} %pad_maximum_fusion.1), channel_id=1, source_target_pairs={{192,0},{193,1},{194,2},{195,3},{196,4},{197,5},{198,6},{199,7},{2... | collective-permute-start | bytes 491528 | tf_op jit(solution)/shard_map/ppermute | solution.py:234
  5.4 31.9 %collective-permute-start.2 = (bf16[192,512]{1,0:T(8,128)(2,1)S(1)}, bf16[192,512]{1,0:T(8,128)(2,1)S(1)}, u32[]{:S(2)}, u32[]{:S(2)}) collective-permute-start(bf16[192,512]{1,0:T(8,128)(2,1)S(1)} %collective-permute-done), channel_id=1, source_target_pairs={{64,256},{65,257},{66,258},{67,259},{68,260},{69,261},{70,262},{71... | collective-permute-start | bytes 589832 | tf_op jit(solution)/shard_map/ppermute | solution.py:234
  6.7 29.3 %collective-permute-start.3 = (bf16[160,512]{1,0:T(8,128)(2,1)S(1)}, bf16[160,512]{1,0:T(8,128)(2,1)S(1)}, u32[]{:S(2)}, u32[]{:S(2)}) collective-permute-start(bf16[160,512]{1,0:T(8,128)(2,1)S(1)} %pad_maximum_fusion), channel_id=1, source_target_pairs={{192,256},{193,257},{194,258},{195,259},{196,260},{197,261},{198,2... | collective-permute-start | bytes 491528 | tf_op jit(solution)/shard_map/ppermute | solution.py:234
  13.3 24.0 %collective-permute-start.5 = (bf16[160,512]{1,0:T(8,128)(2,1)S(1)}, bf16[160,512]{1,0:T(8,128)(2,1)S(1)}, u32[]{:S(2)}, u32[]{:S(2)}) collective-permute-start(bf16[160,512]{1,0:T(8,128)(2,1)S(1)} %collective-permute-done.4), channel_id=1, source_target_pairs={{0,256},{1,257},{2,258},{3,259},{4,260},{5,261},{6,262},{7,263},{8... | collective-permute-start | bytes 491528 | tf_op jit(solution)/shard_map/ppermute | solution.py:234
  31.8 25.1 %copy-start = (bf16[256,512]{1,0:T(8,128)(2,1)S(1)}, bf16[256,512]{1,0:T(8,128)(2,1)}, u32[]{:S(2)}) copy-start(bf16[256,512]{1,0:T(8,128)(2,1)} %refs_0_.1) | copy-start | bytes 786436
  31.8 25.1 %copy-start.1 = (bf16[256,512]{1,0:T(8,128)(2,1)S(1)}, bf16[256,512]{1,0:T(8,128)(2,1)}, u32[]{:S(2)}) copy-start(bf16[256,512]{1,0:T(8,128)(2,1)} %refs_1_.1) | copy-start | bytes 786436
  31.8 25.1 %copy-start.2 = (bf16[256,4096]{1,0:T(8,128)(2,1)S(1)}, bf16[256,4096]{1,0:T(8,128)(2,1)}, u32[]{:S(2)}) copy-start(bf16[256,4096]{1,0:T(8,128)(2,1)} %q_ref.1) | copy-start | bytes 6291460
  31.8 25.0 %collective-permute-start.8 = (bf16[512,512]{1,0:T(8,128)(2,1)}, bf16[512,512]{1,0:T(8,128)(2,1)S(1)}, u32[]{:S(2)}, u32[]{:S(2)}) collective-permute-start(bf16[512,512]{1,0:T(8,128)(2,1)} %pack.1), channel_id=1, source_target_pairs={{0,1},{1,2},{2,3},{3,4},{4,5},{5,6},{6,7},{7,8},{8,9},{9,10},{10,1... | collective-permute-start | bytes 1572872 | tf_op jit(solution)/shard_map/ppermute | solution.py:259
  34.6 10.4 %collective-permute-start.6 = (bf16[512,512]{1,0:T(8,128)(2,1)}, bf16[512,512]{1,0:T(8,128)(2,1)S(1)}, u32[]{:S(2)}, u32[]{:S(2)}) collective-permute-start(bf16[512,512]{1,0:T(8,128)(2,1)} %pack.1), channel_id=1, source_target_pairs={{0,64},{1,65},{2,66},{3,67},{4,68},{5,69},{6,70},{7,71},{8,72},{9,... | collective-permute-start | bytes 1572872 | tf_op jit(solution)/shard_map/ppermute | solution.py:234
  36.0 20.9 %collective-permute-start.1 = (bf16[512,512]{1,0:T(8,128)(2,1)}, bf16[512,512]{1,0:T(8,128)(2,1)S(1)}, u32[]{:S(2)}, u32[]{:S(2)}) collective-permute-start(bf16[512,512]{1,0:T(8,128)(2,1)} %pack.1), channel_id=1, source_target_pairs={{0,32},{1,33},{2,34},{3,35},{4,36},{5,37},{6,38},{7,39},{8,40},{9,... | collective-permute-start | bytes 1572872 | tf_op jit(solution)/shard_map/ppermute | solution.py:234
  45.7 11.2 %collective-permute-start.7 = (bf16[512,512]{1,0:T(8,128)(2,1)S(1)}, bf16[512,512]{1,0:T(8,128)(2,1)S(1)}, u32[]{:S(2)}, u32[]{:S(2)}) collective-permute-start(bf16[512,512]{1,0:T(8,128)(2,1)S(1)} %choose.1.refs_4_), channel_id=1, source_target_pairs={{32,0},{33,1},{34,2},{35,3},{36,4},{37,5},{38,6},{39,7},{40,8},{41... | collective-permute-start | bytes 1572872 | tf_op jit(solution)/shard_map/ppermute | solution.py:234
